TPU v7x, 32 devices: a whole 2x2x4 slice. The times are simulated.
32 devices in a mesh: gz: 8 (over z, x), vert: 4 (over y, core).
Axes of the slice: x: 2, y: 2, z: 4, core: 2. Of those that a mesh axis runs over, the one named last changes fastest.
Arguments:
- estimate: float32 [128, 128, 256], P('gz'), may hold values from 0.5 to 2
- raw_views: bfloat16 [12, 1024, 16, 256], P('vert', 'gz'), may hold values from 0.3 to 3, as said below
- block_dest: int32 [12, 1024], P('vert', 'gz'), may hold values from 0 to 1023, as said below
- lateral_psf: float32 [12, 2, 17], P('vert'), may hold values from 0.05 to 1
- axial_psf: float32 [12, 17], P('vert'), may hold values from 0.05 to 1
Outputs:
- restored: float32 [128, 128, 256], P('gz')
Inputs may be any that keep to these rules, and one draw needn't show every extreme that they name: `block_dest`: for each view the values are a permutation of all block places; a value p lies in slab p // 128. The blocks of one view held by one index of gz go to their slabs in groups of exactly 16 blocks, except one slab that receives exactly 32; every slab receives 128 blocks of each view. `raw_views`: positive intensities.
All inputs are finite; a program needn't handle non-finite values.
Results may differ from a plain program's by a relative error of at most 0.00044.
Values may be sent and summed in bfloat16 or wider, within the bound.
A program may use at most 128 MiB of HBM per device.

v0:
```python
import jax
import jax.numpy as jnp
from jax import lax
from jax.sharding import PartitionSpec as P

VIEWS = 12
ITERS = 2


def extended(shard, sides, width):
    for axis, dim in sides:
        count, length = (lax.axis_size(axis), shard.shape[dim])
        up = [(i, (i + 1) % count) for i in range(count - 1)]
        down = [(j, i) for i, j in up]
        last = lax.slice_in_dim(shard, length - width, length, axis=dim)
        initial = lax.slice_in_dim(shard, 0, width, axis=dim)
        before = lax.ppermute(last, axis, up)
        after = lax.ppermute(initial, axis, down)
        shard = jnp.concatenate([before, shard, after], axis=dim)
    return shard


def normalize(kernel):
    return (kernel / jnp.sum(kernel, axis=-1, keepdims=True)).astype(jnp.bfloat16)


def band_matrix(kernel, extent):
    radius = (kernel.shape[-1] - 1) // 2
    places = jnp.arange(extent)
    offset = places[None, :] - places[:, None] + radius
    chosen = (offset[:, :, None] == jnp.arange(kernel.shape[-1])[None, None, :]).astype(jnp.float32)
    return jnp.einsum("ikw,vw->vik", chosen, kernel.astype(jnp.float32)).astype(jnp.bfloat16)


def axial_matrix(kernel, planes, mirror):
    tap_num = kernel.shape[-1]
    row_ids = jnp.arange(planes)[:, None]
    col_ids = jnp.arange(planes + tap_num - 1)[None, :]
    if mirror:
        offset = row_ids + tap_num - 1 - col_ids
    else:
        offset = col_ids - row_ids
    chosen = (offset[:, :, None] == jnp.arange(tap_num)[None, None, :]).astype(jnp.float32)
    return jnp.einsum("zpw,vw->vzp", chosen, kernel.astype(jnp.float32)).astype(jnp.bfloat16)


def route(raw_views, block_dest, planes, rows_x):
    view_num, blk_num = block_dest.shape
    slab_num = lax.axis_size("gz")
    capacity = 2 * (blk_num // slab_num)
    target = block_dest // blk_num
    placed = block_dest % blk_num
    chosen = (target[:, :, None] == jnp.arange(slab_num)[None, None, :]).astype(jnp.int32)
    before = jnp.sum((jnp.cumsum(chosen, axis=1) - chosen) * chosen, axis=2)
    slot_index = target * capacity + before
    view_ids = jnp.arange(view_num)[:, None]
    tail = raw_views.shape[2:]
    outgoing = (
        jnp.zeros((view_num, slab_num * capacity) + tail, jnp.bfloat16)
        .at[view_ids, slot_index]
        .set(raw_views)
    )
    labels = (
        jnp.full((view_num, slab_num * capacity), blk_num, jnp.int32)
        .at[view_ids, slot_index]
        .set(placed)
    )
    outgoing = outgoing.reshape((view_num, slab_num, capacity) + tail)
    labels = labels.reshape(view_num, slab_num, capacity)
    incoming, landed = (
        lax.all_to_all(outgoing, "gz", split_axis=1, concat_axis=1, tiled=True),
        lax.all_to_all(labels, "gz", split_axis=1, concat_axis=1, tiled=True),
    )
    incoming = incoming.reshape((view_num, slab_num * capacity) + tail)
    landed = landed.reshape(view_num, slab_num * capacity)
    blocks = (
        jnp.zeros(raw_views.shape, jnp.bfloat16).at[view_ids, landed].set(incoming, mode="drop")
    )
    return blocks.reshape(view_num, planes, rows_x, tail[1])


def body(estimate, raw_views, block_dest, lateral_psf, axial_psf):
    planes, rows_x, rows_y = estimate.shape
    observed = route(raw_views, block_dest, planes, rows_x)
    along_x = normalize(lateral_psf[:, 0])
    along_y = normalize(lateral_psf[:, 1])
    depth = normalize(axial_psf)
    radius = (axial_psf.shape[1] - 1) // 2
    mat_x = band_matrix(along_x, rows_x)
    mat_y = band_matrix(along_y, rows_y)
    back_matrix = axial_matrix(depth, planes, True)
    front_matrix = axial_matrix(depth, planes, False)
    for iteration in range(ITERS):
        lowered = estimate.astype(jnp.bfloat16)
        widened = extended(lowered, (("gz", 0),), radius)
        first = jnp.einsum(
            "vzp,pxy->vzxy", front_matrix, widened, preferred_element_type=jnp.float32
        ).astype(jnp.bfloat16)
        second = jnp.einsum(
            "vik,vzky->vziy", mat_x, first, preferred_element_type=jnp.float32
        ).astype(jnp.bfloat16)
        blurred = jnp.einsum("vzxl,vjl->vzxj", second, mat_y, preferred_element_type=jnp.float32)
        ratio = (observed.astype(jnp.float32) / blurred).astype(jnp.bfloat16)
        third = jnp.einsum(
            "vzxj,vjl->vzxl", ratio, mat_y, preferred_element_type=jnp.float32
        ).astype(jnp.bfloat16)
        fourth = jnp.einsum(
            "vik,vziy->vzky", mat_x, third, preferred_element_type=jnp.float32
        ).astype(jnp.bfloat16)
        spread = extended(fourth, (("gz", 1),), radius)
        partial_back = jnp.einsum(
            "vzp,vpxy->zxy", back_matrix, spread, preferred_element_type=jnp.float32
        )
        correction = lax.psum(partial_back, "vert")
        estimate = estimate * correction / VIEWS
    return estimate


def solution(mesh):
    return jax.shard_map(
        body,
        mesh=mesh,
        in_specs=(
            P("gz", None, None),
            P("vert", "gz", None, None),
            P("vert", "gz"),
            P("vert", None, None),
            P("vert", None),
        ),
        out_specs=P("gz", None, None),
        check_vma=False,
    )
```

profile of v0, /device:TPU:0, one launch (start us, length us, event | category | flops | bytes accessed | tf_op | source)
XLA Modules:
  0.0 670.0 jit_solution(6598337202948744321)
XLA Ops:
  7.8 19.7 %scatter_fusion = s32[3,256]{1,0:T(4,128)S(1)} fusion(s32[3,256]{1,0:T(4,128)S(1)} %broadcast.99, s32[384]{0:T(512)S(1)} %fusion.61, s32[384]{0:T(512)S(1)} %get-tuple-element.17), kind=kCustom, calls=%fused_computation | custom fusion | bytes 7680 | tf_op jit(solution)/shard_map/scatter | solution.py:66
  28.2 7.3 %all-to-all-start = ((s32[3,8,32]{2,0,1:T(4,128)}), s32[3,8,32]{2,0,1:T(4,128)S(1)}, u32[]{:S(2)}, u32[]{:S(2)}) async-start(s32[3,8,32]{2,0,1:T(4,128)} %copy.75), calls=%async_computation | async-start | bytes 32768 | tf_op jit(solution)/shard_map/all_to_all | solution.py:72
  35.5 3.1 broadcast_in_dim.14
  38.6 40.4 %scatter_fusion.1 = bf16[3,256,16,256]{3,2,1,0:T(8,128)(2,1)} fusion(bf16[3,256,16,256]{3,2,1,0:T(8,128)(2,1)} %broadcast_in_dim.14, s32[384]{0:T(512)S(1)} %fusion.61, bf16[384,16,256]{2,1,0:T(8,128)(2,1)S(1)} %bitcast.104), kind=kCustom, calls=%fused_computation.1 | custom fusion | bytes 9440256 | tf_op jit(solution)/shard_map/scatter | solution.py:61
  79.0 6.0 copy.77
  85.0 6.2 all-to-all-start.1
  92.5 4.7 collective-permute-start
  101.0 54.4 %collective-permute-done = bf16[8,128,256]{2,0,1:T(8,128)(2,1)} collective-permute-done((bf16[8,128,256]{2,0,1:T(8,128)(2,1)S(1)}, bf16[8,128,256]{2,0,1:T(8,128)(2,1)}, u32[]{:S(2)}, u32[]{:S(2)}) %collective-permute-start) | collective-permute-done | bytes 524320 | tf_op jit(solution)/shard_map/ppermute | solution.py:17
  155.3 3.8 convolution_convert_fusion.1
  159.2 7.0 %fusion.5 = f32[3,16,128,256]{3,2,1,0:T(8,128)} fusion(bf16[3,16,128,256]{3,1,2,0:T(8,128)(2,1)} %convolution_convert_fusion.1, bf16[3,128,128]{2,0,1:T(4,128)(2,1)S(1)} %fusion.42, bf16[3,256,256]{2,0,1:T(4,128)(2,1)S(1)} %fusion.2), kind=kOutput, calls=%fused_computation.13 | convolution fusion | flops 1209532416 | bytes 9928704 | tf_op jit(solution)/shard_map/vzxl,vjl->vzxj/dot_general | solution.py:102
  166.2 64.7 %all-to-all-done.1 = bf16[3,8,32,16,256]{4,3,2,0,1:T(8,128)(2,1)} async-done(((bf16[3,8,32,16,256]{4,3,2,0,1:T(8,128)(2,1)}), bf16[3,8,32,16,256]{4,3,2,0,1:T(8,128)(2,1)}, u32[]{:S(2)}, u32[]{:S(2)}) %all-to-all-start.1) | async-done | bytes 6291488 | tf_op jit(solution)/shard_map/all_to_all | solution.py:71
  230.9 6.0 copy.78
  237.1 52.5 %scatter_fusion.2 = bf16[3,128,16,256]{3,2,1,0:T(8,128)(2,1)S(1)} fusion(bf16[3,128,16,256]{3,2,1,0:T(8,128)(2,1)S(1)} %broadcast_in_dim.10, s32[768]{0:T(1024)S(1)} %reshape.130, bf16[768,16,256]{2,1,0:T(8,128)(2,1)} %bitcast.103), kind=kCustom, calls=%fused_computation.2 | custom fusion | bytes 18880512 | tf_op jit(solution)/shard_map/scatter | solution.py:77
  289.6 6.5 fusion
  296.1 5.5 convert_bitcast_fusion.1
  303.8 11.0 %collective-permute-start.2 = (bf16[3,8,128,256]{2,3,1,0:T(8,128)(2,1)S(1)}, bf16[3,8,128,256]{2,3,1,0:T(8,128)(2,1)S(1)}, u32[]{:S(2)}, u32[]{:S(2)}) collective-permute-start(bf16[3,8,128,256]{2,3,1,0:T(8,128)(2,1)S(1)} %get-tuple-element.9), channel_id=1, source_target_pairs={{0,4},{4,8},{8,12},{12,16},{16,20},{20,24},{24,28},{1,5},{5,9},{9,... | collective-permute-start | bytes 4718600 | tf_op jit(solution)/shard_map/ppermute | solution.py:17
  316.6 64.6 %collective-permute-done.2 = bf16[3,8,128,256]{2,3,1,0:T(8,128)(2,1)S(1)} collective-permute-done((bf16[3,8,128,256]{2,3,1,0:T(8,128)(2,1)S(1)}, bf16[3,8,128,256]{2,3,1,0:T(8,128)(2,1)S(1)}, u32[]{:S(2)}, u32[]{:S(2)}) %collective-permute-start.2) | collective-permute-done | bytes 1572896 | tf_op jit(solution)/shard_map/ppermute | solution.py:17
  384.4 9.2 %copy.86 = bf16[3,32,128,256]{3,1,0,2:T(8,128)(2,1)} copy(bf16[3,32,128,256]{2,3,1,0:T(8,128)(2,1)} %pad_maximum_fusion) | data formatting | bytes 12582912 | tf_op jit(solution)/shard_map/concatenate | solution.py:19
  393.6 5.2 convolution_bitcast_fusion.1
  398.8 65.1 %all-reduce.3.cloned.1.call-done = f32[16,128,256]{2,0,1:T(8,128)} async-done(((f32[16,128,256]{2,0,1:T(8,128)}), f32[16,128,256]{2,0,1:T(8,128)}) %all-reduce.3.cloned.1.call-update) | async-done | bytes 2097168 | tf_op jit(solution)/shard_map/psum | solution.py:114
  463.9 3.6 fusion.44
  467.6 3.4 collective-permute-start.4
  472.3 21.0 %collective-permute-done.4 = bf16[8,128,256]{2,0,1:T(8,128)(2,1)S(1)} collective-permute-done((bf16[8,128,256]{2,0,1:T(8,128)(2,1)S(1)}, bf16[8,128,256]{2,0,1:T(8,128)(2,1)S(1)}, u32[]{:S(2)}, u32[]{:S(2)}) %collective-permute-start.4) | collective-permute-done | bytes 524320 | tf_op jit(solution)/shard_map/ppermute | solution.py:17
  495.9 7.2 %fusion.3 = f32[3,16,128,256]{3,2,1,0:T(8,128)} fusion(bf16[3,16,128,256]{3,1,2,0:T(8,128)(2,1)} %convolution_convert_fusion, bf16[3,128,128]{2,0,1:T(4,128)(2,1)S(1)} %fusion.42, bf16[3,256,256]{2,0,1:T(4,128)(2,1)} %copy-done.4), kind=kOutput, calls=%fused_computation.11 | convolution fusion | flops 1209532416 | bytes 9928704 | tf_op jit(solution)/shard_map/vzxl,vjl->vzxj/dot_general | solution.py:102
  503.1 6.5 fusion.1
  509.6 3.8 convert_bitcast_fusion
  513.7 4.5 collective-permute-start.6
  519.7 64.8 %collective-permute-done.6 = bf16[3,8,128,256]{2,3,1,0:T(8,128)(2,1)S(1)} collective-permute-done((bf16[3,8,128,256]{2,3,1,0:T(8,128)(2,1)S(1)}, bf16[3,8,128,256]{2,3,1,0:T(8,128)(2,1)S(1)}, u32[]{:S(2)}, u32[]{:S(2)}) %collective-permute-start.6) | collective-permute-done | bytes 1572896 | tf_op jit(solution)/shard_map/ppermute | solution.py:17
  587.6 9.2 %copy.91 = bf16[3,32,128,256]{3,1,0,2:T(8,128)(2,1)} copy(bf16[3,32,128,256]{2,3,1,0:T(8,128)(2,1)} %pad_maximum_fusion.1) | data formatting | bytes 12582912 | tf_op jit(solution)/shard_map/concatenate | solution.py:19
  596.8 5.2 convolution_bitcast_fusion
  602.0 54.8 %all-reduce.5.cloned.1.call-done = f32[16,128,256]{2,0,1:T(8,128)} async-done(((f32[16,128,256]{2,0,1:T(8,128)}), f32[16,128,256]{2,0,1:T(8,128)}) %all-reduce.5.cloned.1.call-update) | async-done | bytes 2097168 | tf_op jit(solution)/shard_map/psum | solution.py:114
  656.8 3.8 multiply_multiply_fusion
  (60 shorter events, 26.0 us)
Async XLA Ops:
  28.2 56.8 %all-to-all-start = ((s32[3,8,32]{2,0,1:T(4,128)}), s32[3,8,32]{2,0,1:T(4,128)S(1)}, u32[]{:S(2)}, u32[]{:S(2)}) async-start(s32[3,8,32]{2,0,1:T(4,128)} %copy.75), calls=%async_computation | async-start | bytes 32768 | tf_op jit(solution)/shard_map/all_to_all | solution.py:72
  35.5 3.2 copy-start.3
  85.0 6.2 copy-start
  85.0 145.8 %all-to-all-start.1 = ((bf16[3,8,32,16,256]{4,3,2,0,1:T(8,128)(2,1)}), bf16[3,8,32,16,256]{4,3,2,0,1:T(8,128)(2,1)}, u32[]{:S(2)}, u32[]{:S(2)}) async-start(bf16[3,8,32,16,256]{4,3,2,0,1:T(8,128)(2,1)} %copy.77), calls=%async_computation.1 | async-start | bytes 12582912 | tf_op jit(solution)/shard_map/all_to_all | solution.py:71
  91.2 7.5 %copy-start.6 = (f32[3,17]{1,0:T(4,128)S(1)}, f32[3,17]{1,0:T(4,128)}, u32[]{:S(2)}) copy-start(f32[3,17]{1,0:T(4,128)} %param.9) | copy-start | bytes 616
  91.2 7.6 %copy-start.5 = (f32[3,2,17]{2,1,0:T(2,128)S(1)}, f32[3,2,17]{2,1,0:T(2,128)}, u32[]{:S(2)}) copy-start(f32[3,2,17]{2,1,0:T(2,128)} %param.8) | copy-start | bytes 1228
  91.2 372.7 %all-reduce.3.cloned.1.call-start = ((), (), s32[]{:S(2)}) async-start(), calls=%async_computation.2 | async-start | bytes 4194304 | tf_op jit(solution)/shard_map/psum | solution.py:114
  92.5 62.9 %collective-permute-start = (bf16[8,128,256]{2,0,1:T(8,128)(2,1)S(1)}, bf16[8,128,256]{2,0,1:T(8,128)(2,1)}, u32[]{:S(2)}, u32[]{:S(2)}) collective-permute-start(bf16[8,128,256]{2,0,1:T(8,128)(2,1)S(1)} %get-tuple-element.13), channel_id=1, source_target_pairs={{0,4},{4,8},{8,12},{12,16},{16,20},{20,24},{24,28},{1,5},{5,9},{9,... | collective-permute-start | bytes 1572872 | tf_op jit(solution)/shard_map/ppermute | solution.py:17
  97.2 58.1 %collective-permute-start.1 = (bf16[8,128,256]{2,0,1:T(8,128)(2,1)S(1)}, bf16[8,128,256]{2,0,1:T(8,128)(2,1)}, u32[]{:S(2)}, u32[]{:S(2)}) collective-permute-start(bf16[8,128,256]{2,0,1:T(8,128)(2,1)S(1)} %get-tuple-element.14), channel_id=1, source_target_pairs={{4,0},{8,4},{12,8},{16,12},{20,16},{24,20},{28,24},{5,1},{9,5},{13... | collective-permute-start | bytes 1572872 | tf_op jit(solution)/shard_map/ppermute | solution.py:18
  100.9 65.3 %copy-start.4 = (bf16[3,256,256]{2,0,1:T(4,128)(2,1)}, bf16[3,256,256]{2,0,1:T(4,128)(2,1)S(1)}, u32[]{:S(2)}) copy-start(bf16[3,256,256]{2,0,1:T(4,128)(2,1)S(1)} %fusion.2) | copy-start | bytes 1179652
  301.5 79.8 %copy-start.2 = (bf16[3,16,128,256]{2,3,1,0:T(8,128)(2,1)S(1)}, bf16[3,16,128,256]{2,3,1,0:T(8,128)(2,1)}, u32[]{:S(2)}) copy-start(bf16[3,16,128,256]{2,3,1,0:T(8,128)(2,1)} %convert_bitcast_fusion.1) | copy-start | bytes 9437188
  303.8 77.5 %collective-permute-start.2 = (bf16[3,8,128,256]{2,3,1,0:T(8,128)(2,1)S(1)}, bf16[3,8,128,256]{2,3,1,0:T(8,128)(2,1)S(1)}, u32[]{:S(2)}, u32[]{:S(2)}) collective-permute-start(bf16[3,8,128,256]{2,3,1,0:T(8,128)(2,1)S(1)} %get-tuple-element.9), channel_id=1, source_target_pairs={{0,4},{4,8},{8,12},{12,16},{16,20},{20,24},{24,28},{1,5},{5,9},{9,... | collective-permute-start | bytes 4718600 | tf_op jit(solution)/shard_map/ppermute | solution.py:17
  314.8 66.5 %collective-permute-start.3 = (bf16[3,8,128,256]{2,3,1,0:T(8,128)(2,1)S(1)}, bf16[3,8,128,256]{2,3,1,0:T(8,128)(2,1)S(1)}, u32[]{:S(2)}, u32[]{:S(2)}) collective-permute-start(bf16[3,8,128,256]{2,3,1,0:T(8,128)(2,1)S(1)} %get-tuple-element.10), channel_id=1, source_target_pairs={{4,0},{8,4},{12,8},{16,12},{20,16},{24,20},{28,24},{5,1},{9,5},{13... | collective-permute-start | bytes 4718600 | tf_op jit(solution)/shard_map/ppermute | solution.py:18
  398.8 258.0 %all-reduce.5.cloned.1.call-start = ((), (), s32[]{:S(2)}) async-start(), calls=%async_computation.3 | async-start | bytes 4194304 | tf_op jit(solution)/shard_map/psum | solution.py:114
  467.6 25.7 %collective-permute-start.4 = (bf16[8,128,256]{2,0,1:T(8,128)(2,1)S(1)}, bf16[8,128,256]{2,0,1:T(8,128)(2,1)S(1)}, u32[]{:S(2)}, u32[]{:S(2)}) collective-permute-start(bf16[8,128,256]{2,0,1:T(8,128)(2,1)S(1)} %get-tuple-element.11), channel_id=1, source_target_pairs={{0,4},{4,8},{8,12},{12,16},{16,20},{20,24},{24,28},{1,5},{5,9},{9,... | collective-permute-start | bytes 1572872 | tf_op jit(solution)/shard_map/ppermute | solution.py:17
  471.0 22.3 %collective-permute-start.5 = (bf16[8,128,256]{2,0,1:T(8,128)(2,1)S(1)}, bf16[8,128,256]{2,0,1:T(8,128)(2,1)S(1)}, u32[]{:S(2)}, u32[]{:S(2)}) collective-permute-start(bf16[8,128,256]{2,0,1:T(8,128)(2,1)S(1)} %get-tuple-element.12), channel_id=1, source_target_pairs={{4,0},{8,4},{12,8},{16,12},{20,16},{24,20},{28,24},{5,1},{9,5},{13... | collective-permute-start | bytes 1572872 | tf_op jit(solution)/shard_map/ppermute | solution.py:18
  513.7 70.8 %collective-permute-start.6 = (bf16[3,8,128,256]{2,3,1,0:T(8,128)(2,1)S(1)}, bf16[3,8,128,256]{2,3,1,0:T(8,128)(2,1)S(1)}, u32[]{:S(2)}, u32[]{:S(2)}) collective-permute-start(bf16[3,8,128,256]{2,3,1,0:T(8,128)(2,1)S(1)} %get-tuple-element.7), channel_id=1, source_target_pairs={{0,4},{4,8},{8,12},{12,16},{16,20},{20,24},{24,28},{1,5},{5,9},{9,... | collective-permute-start | bytes 4718600 | tf_op jit(solution)/shard_map/ppermute | solution.py:17
  518.2 66.3 %collective-permute-start.7 = (bf16[3,8,128,256]{2,3,1,0:T(8,128)(2,1)S(1)}, bf16[3,8,128,256]{2,3,1,0:T(8,128)(2,1)S(1)}, u32[]{:S(2)}, u32[]{:S(2)}) collective-permute-start(bf16[3,8,128,256]{2,3,1,0:T(8,128)(2,1)S(1)} %get-tuple-element.8), channel_id=1, source_target_pairs={{4,0},{8,4},{12,8},{16,12},{20,16},{24,20},{28,24},{5,1},{9,5},{13... | collective-permute-start | bytes 4718600 | tf_op jit(solution)/shard_map/ppermute | solution.py:18
  602.0 54.8 %copy-start.1 = (f32[16,128,256]{2,1,0:T(8,128)S(1)}, f32[16,128,256]{2,1,0:T(8,128)}, u32[]{:S(2)}) copy-start(f32[16,128,256]{2,1,0:T(8,128)} %param.5) | copy-start | bytes 6291460
Sparse Core Ops, SparseCore 0:
  398.9 64.9 all-reduce.2
  602.1 54.6 all-reduce.4
where the time goes:
time: 673 us; the launch traced here: 670 us
  waiting for transfers between devices  389 us (58%)
  local copies, waits for them, and re-layouts  154 us (23%)
  starting transfers between devices  42.9 us (6%)
  matrix products  42.3 us (6%)
  other arithmetic  28.2 us (4%)
  between operations  13.7 us (2%)
    ppermute x4, waiting for transfers between devices, extended(): before = lax.ppermute(last, axis, up)  205 us
    psum x2, waiting for transfers between devices, body(): correction = lax.psum(partial_back, 'vert')  120 us
    all_to_all x1, waiting for transfers between devices, route(): lax.all_to_all(outgoing, 'gz', split_axis=1, concat_axis=1, tiled=True)  64.7 us
    scatter x1, local copies, waits for them, and re-layouts, route(): jnp.zeros(raw_views.shape, jnp.bfloat16).at[view_ids, landed]  52.5 us
    scatter x1, local copies, waits for them, and re-layouts, route(): outgoing = jnp.zeros((view_num, slab_num * capacity) + tail, jnp.bfloat16...  40.4 us
    ppermute x4, starting transfers between devices, extended(): before = lax.ppermute(last, axis, up)  23.6 us
    scatter x1, local copies, waits for them, and re-layouts, route(): labels = jnp.full((view_num, slab_num * capacity), blk_num, jnp.int32).at...  19.7 us
    concatenate x2, local copies, waits for them, and re-layouts, extended(): shard = jnp.concatenate([before, shard, after], axis=dim)  18.3 us
  transfers between devices with their start and end apart: 12, of which 7 were waited for; matrix products, arithmetic and copies ran while one was open for 10% of the time, Pallas kernels for 0%

commit v1 on v0

v1 whole, which is shorter than its diff:
```python
import jax
import jax.numpy as jnp
from jax import lax
from jax.experimental import pallas as pl
from jax.experimental.pallas import tpu as pltpu
from jax.sharding import PartitionSpec as P

VIEWS = 12
ITERS = 2
VMEM_LIMIT = 48 * 1024 * 1024


def shift(array, axis, step):
    count = lax.axis_size(axis)
    if step > 0:
        pairs = [(i, i + 1) for i in range(count - 1)]
    else:
        pairs = [(i + 1, i) for i in range(count - 1)]
    return lax.ppermute(array, axis, pairs)


def normalize(kernel):
    return (kernel / jnp.sum(kernel, axis=-1, keepdims=True)).astype(jnp.bfloat16)


def band_matrix(kernel, extent):
    radius = (kernel.shape[-1] - 1) // 2
    places = jnp.arange(extent)
    offset = places[None, :] - places[:, None] + radius
    chosen = (offset[:, :, None] == jnp.arange(kernel.shape[-1])[None, None, :]).astype(jnp.float32)
    return jnp.einsum("ikw,vw->vik", chosen, kernel.astype(jnp.float32)).astype(jnp.bfloat16)


def axial_matrix(kernel, planes):
    tap_num = kernel.shape[-1]
    row_ids = jnp.arange(planes)[:, None]
    col_ids = jnp.arange(planes + tap_num - 1)[None, :]
    offset = col_ids - row_ids
    chosen = (offset[:, :, None] == jnp.arange(tap_num)[None, None, :]).astype(jnp.float32)
    return jnp.einsum("zpw,vw->vzp", chosen, kernel.astype(jnp.float32)).astype(jnp.bfloat16)


def pack_kernel(source, raw, packed, extra):
    slabs, views, group = packed.shape[:3]

    for v in range(views):

        @pl.loop(0, slabs)
        def _(s):
            for k in range(group):
                packed[s, v, k] = raw[v, source[v, s * group + k]]

        for k in range(group):
            extra[v, k] = raw[v, source[v, slabs * group + k]]


def pack(source, raw, slabs, group):
    views, _, band, rows_y = raw.shape
    vmem = pl.BlockSpec(memory_space=pltpu.VMEM)
    return pl.pallas_call(
        pack_kernel,
        out_shape=(
            jax.ShapeDtypeStruct((slabs, views, group, band, rows_y), raw.dtype),
            jax.ShapeDtypeStruct((views, group, band, rows_y), raw.dtype),
        ),
        in_specs=[pl.BlockSpec(memory_space=pltpu.SMEM), vmem],
        out_specs=(vmem, vmem),
        compiler_params=pltpu.CompilerParams(vmem_limit_bytes=VMEM_LIMIT),
        name="pack",
    )(source, raw)


def place_kernel(source, main, extra, blocks):
    views, num = blocks.shape[:2]
    unroll = 8

    for v in range(views):

        @pl.loop(0, num // unroll)
        def _(step):
            for k in range(unroll):
                q = step * unroll + k
                chosen = source[v, q]
                slab = chosen // 65536
                late = (chosen // 256) % 256
                slot = chosen % 256
                early_block = main[slab, v, slot]
                late_block = extra[slab, v, slot]
                blocks[v, q] = jnp.where(late == 1, late_block, early_block)


def place(source, main, extra):
    slabs, views, group, band, rows_y = main.shape
    vmem = pl.BlockSpec(memory_space=pltpu.VMEM)
    return pl.pallas_call(
        place_kernel,
        out_shape=jax.ShapeDtypeStruct((views, slabs * group, band, rows_y), main.dtype),
        in_specs=[pl.BlockSpec(memory_space=pltpu.SMEM), vmem, vmem],
        out_specs=vmem,
        compiler_params=pltpu.CompilerParams(vmem_limit_bytes=VMEM_LIMIT),
        name="place",
    )(source, main, extra)


def slots_of(dest, blk_num, slabs):
    target = dest // blk_num
    placed = dest % blk_num
    order = jnp.arange(blk_num)
    earlier = order[None, :] < order[:, None]
    same = (target[..., None, :] == target[..., :, None]) & earlier
    return target, placed, jnp.sum(same.astype(jnp.int32), axis=-1)


def route(raw_views, block_dest):
    view_num, blk_num = block_dest.shape
    slabs = lax.axis_size("gz")
    group = blk_num // slabs
    me = lax.axis_index("gz")
    target, placed, rank = slots_of(block_dest, blk_num, slabs)
    slot = jnp.where(rank < group, target * group + rank, slabs * group + rank - group)
    hit = slot[:, None, :] == jnp.arange((slabs + 1) * group)[None, :, None]
    source = jnp.sum(jnp.where(hit, jnp.arange(blk_num)[None, None, :], 0), axis=-1)
    packed, extra = pack(source, raw_views, slabs, group)
    main = lax.all_to_all(packed, "gz", split_axis=0, concat_axis=0, tiled=True)
    late = lax.all_gather(extra, "gz", axis=0)
    dests = lax.all_gather(block_dest, "gz", axis=0)
    target, placed, rank = slots_of(dests, blk_num, slabs)
    slab_ids = jnp.arange(slabs)[:, None, None]
    code = slab_ids * 65536 + jnp.where(rank < group, rank, 256 + rank - group)
    code = jnp.where(target == me, code, 0)
    code = jnp.swapaxes(code, 0, 1).reshape(view_num, slabs * blk_num)
    where = jnp.where(target == me, placed, blk_num)
    where = jnp.swapaxes(where, 0, 1).reshape(view_num, slabs * blk_num)
    hit = where[:, None, :] == jnp.arange(blk_num)[None, :, None]
    inverse = jnp.sum(jnp.where(hit, code[:, None, :], 0), axis=-1)
    return place(inverse, main, late)


def with_halo(quarter, radius):
    planes = quarter.shape[0]
    before = shift(quarter[planes - radius:], "gz", 1)
    after = shift(quarter[:radius], "gz", -1)
    return before, after


def body(estimate, raw_views, block_dest, lateral_psf, axial_psf):
    planes, rows_x, rows_y = estimate.shape
    along_x = normalize(lateral_psf[:, 0])
    along_y = normalize(lateral_psf[:, 1])
    depth = normalize(axial_psf)
    radius = (axial_psf.shape[1] - 1) // 2
    mat_x = band_matrix(along_x, rows_x)
    mat_y = band_matrix(along_y, rows_y)
    front_matrix = axial_matrix(depth, planes)
    parts = lax.axis_size("vert")
    rows_q = rows_x // parts
    mine = lax.axis_index("vert") * rows_q
    held = lax.dynamic_slice_in_dim(estimate, mine, rows_q, axis=1)
    before, after = with_halo(held.astype(jnp.bfloat16), radius)
    sides = lax.all_gather(jnp.concatenate([before, after], axis=0), "vert", axis=1, tiled=True)
    widened = jnp.concatenate(
        [sides[:radius], estimate.astype(jnp.bfloat16), sides[radius:]], axis=0
    )
    observed = route(raw_views, block_dest).reshape(-1, planes, rows_x, rows_y)
    for iteration in range(ITERS):
        first = jnp.einsum(
            "vzp,pxy->vzxy", front_matrix, widened, preferred_element_type=jnp.float32
        ).astype(jnp.bfloat16)
        second = jnp.einsum(
            "vik,vzky->vziy", mat_x, first, preferred_element_type=jnp.float32
        ).astype(jnp.bfloat16)
        blurred = jnp.einsum("vzxl,vjl->vzxj", second, mat_y, preferred_element_type=jnp.float32)
        ratio = (observed.astype(jnp.float32) / blurred).astype(jnp.bfloat16)
        third = jnp.einsum(
            "vzxj,vjl->vzxl", ratio, mat_y, preferred_element_type=jnp.float32
        ).astype(jnp.bfloat16)
        fourth = jnp.einsum(
            "vik,vziy->vzky", mat_x, third, preferred_element_type=jnp.float32
        ).astype(jnp.bfloat16)
        partial_back = jnp.einsum(
            "vzp,vzxy->pxy", front_matrix, fourth, preferred_element_type=jnp.float32
        )
        summed = lax.psum_scatter(partial_back, "vert", scatter_dimension=1, tiled=True)
        below = shift(summed[planes + radius:], "gz", 1)
        above = shift(summed[:radius], "gz", -1)
        correction = summed[radius:planes + radius] + jnp.concatenate([below, above], axis=0)
        held = held * correction / VIEWS
        if iteration < ITERS - 1:
            lowered = held.astype(jnp.bfloat16)
            before, after = with_halo(lowered, radius)
            widened = lax.all_gather(
                jnp.concatenate([before, lowered, after], axis=0), "vert", axis=1, tiled=True
            )
    return lax.all_gather(held, "vert", axis=1, tiled=True)


def solution(mesh):
    return jax.shard_map(
        body,
        mesh=mesh,
        in_specs=(
            P("gz", None, None),
            P("vert", "gz", None, None),
            P("vert", "gz"),
            P("vert", None, None),
            P("vert", None),
        ),
        out_specs=P("gz", None, None),
        check_vma=False,
    )
```

time: 673 us -> 428 us (0.64)
  waiting for transfers between devices: 389 us -> 165 us
  local copies, waits for them, and re-layouts: 154 us -> 24.6 us
  blocking collectives: 0 us -> 122 us
  starting transfers between devices: 42.9 us -> 27.4 us
  Pallas kernels: 0 us -> 13.3 us
  other arithmetic: 28.2 us -> 18.1 us
    ppermute x8, waiting for transfers between devices: 205 us -> 31.6 us  [shift(): return lax.ppermute(array, axis, pairs)]
    all_gather x0 -> x1, blocking collectives: none -> 122 us  [route(): dests = lax.all_gather(block_dest, 'gz', axis=0)]
    psum x2 -> x0, waiting for transfers between devices: 120 us -> none  [body(): correction = lax.psum(partial_back, 'vert')]
    scatter x3 -> x0, local copies, waits for them, and re-layouts: 113 us -> none  [the longest x1 52.5 us: route(): jnp.zeros(raw_views.shape, jnp.bfloat16).at[view_ids, landed]]
    reduce_scatter x0 -> x2, waiting for transfers between devices: none -> 86.5 us  [body(): lax.psum_scatter(partial_back, 'vert', scatter_dimension=1, tiled=True)]
    all_to_all x2 -> x1, waiting for transfers between devices: 64.7 us -> 0.01 us  [route(): main = lax.all_to_all(packed, 'gz', split_axis=0, concat_axis=0, tiled=True)]
    all_gather x0 -> x4, waiting for transfers between devices: none -> 46.5 us  [the longest x1 23.8 us: body(): return lax.all_gather(held, 'vert', axis=1, tiled=True)]
    concatenate x3 -> x0, local copies, waits for them, and re-layouts: 18.3 us -> none  [the longest x2 18.3 us: extended(): shard = jnp.concatenate([before, shard, after], axis=dim)]
  transfers between devices with their start and end apart: 12 -> 15, of which waited for: 7 -> 10; matrix products, arithmetic and copies ran while one was open for 10% -> 5% of each run, Pallas kernels for 0% -> 1%
where the time goes in v1:
time: 428 us; the launch traced here: 427 us
  waiting for transfers between devices  165 us (39%)
  blocking collectives  122 us (29%)
  matrix products  43.3 us (10%)
  starting transfers between devices  27.4 us (6%)
  local copies, waits for them, and re-layouts  24.6 us (6%)
  other arithmetic  18.1 us (4%)
  between operations  13.7 us (3%)
  Pallas kernels  13.3 us (3%)
    all_gather x1, blocking collectives, route(): dests = lax.all_gather(block_dest, 'gz', axis=0)  122 us
    reduce_scatter x2, waiting for transfers between devices, body(): lax.psum_scatter(partial_back, 'vert', scatter_dimension=1, tiled=True)  86.5 us
    ppermute x8, waiting for transfers between devices, shift(): return lax.ppermute(array, axis, pairs)  31.6 us
    all_gather x1, waiting for transfers between devices, body(): return lax.all_gather(held, 'vert', axis=1, tiled=True)  23.8 us
    all_gather x1, waiting for transfers between devices, body(): lax.all_gather(jnp.concatenate([before, lowered, after], axis=0), 'vert',...  22.7 us
    ppermute x8, starting transfers between devices, shift(): return lax.ppermute(array, axis, pairs)  21.2 us
    dot_general x2, matrix products, body(): jnp.einsum('vzxl,vjl->vzxj', second, mat_y, preferred_element_type=jnp.fl...  14.4 us
    dot_general x2, matrix products, body(): jnp.einsum('vik,vziy->vzky', mat_x, third, preferred_element_type=jnp.flo...  10.9 us
  transfers between devices with their start and end apart: 15, of which 10 were waited for; matrix products, arithmetic and copies ran while one was open for 5% of the time, Pallas kernels for 1%

profile of v1, /device:TPU:0, one launch (start us, length us, event | category | flops | bytes accessed | tf_op | source)
XLA Modules:
  0.0 427.3 jit_solution(1977053359296687360)
XLA Ops:
  6.5 2.8 copy.64
  9.4 4.8 %collective-permute-start = (bf16[8,32,256]{2,0,1:T(8,128)(2,1)S(1)}, bf16[8,32,256]{2,0,1:T(8,128)(2,1)S(1)}, u32[]{:S(2)}, u32[]{:S(2)}) collective-permute-start(bf16[8,32,256]{2,0,1:T(8,128)(2,1)S(1)} %get-tuple-element.24), channel_id=1, source_target_pairs={{0,4},{4,8},{8,12},{12,16},{16,20},{20,24},{24,28},{1,5},{5,9},{9,... | collective-permute-start | bytes 393224 | tf_op jit(solution)/shard_map/ppermute | solution.py:19
  17.0 4.1 collective-permute-done.1
  22.4 4.7 %pack.1 = (bf16[8,3,16,16,256]{4,3,2,1,0:T(8,128)(2,1)}, bf16[3,16,16,256]{3,2,1,0:T(8,128)(2,1)}) custom-call(s32[3,144]{1,0:T(4,128)S(1)} %select_reduce_fusion.1.source, bf16[3,128,16,256]{3,2,1,0:T(8,128)(2,1)} %raw.1), custom_call_target="tpu_custom_call" | custom-call | tf_op jit(solution)/shard_map/pack/pallas_call | solution.py:60
  27.1 5.7 %all-to-all-start = ((bf16[8,3,16,16,256]{4,3,2,1,0:T(8,128)(2,1)}), bf16[8,3,16,16,256]{4,3,2,1,0:T(8,128)(2,1)S(1)}, u32[]{:S(2)}, u32[]{:S(2)}) async-start(bf16[8,3,16,16,256]{4,3,2,1,0:T(8,128)(2,1)} %get-tuple-element.7), calls=%async_computation | async-start | bytes 6291456 | tf_op jit(solution)/shard_map/all_to_all | solution.py:124
  33.7 3.7 copy.122
  37.5 121.5 %all-gather.2 = s32[8,3,128]{2,1,0:T(4,128)S(1)} all-gather(s32[1,3,128]{2,1,0:T(4,128)S(1)} %bitcast.99), channel_id=2, replica_groups=mesh['gz'=8,'vert'=4] {'gz'}, dimensions={0}, use_global_device_ids=true | all-gather | bytes 13824 | tf_op jit(solution)/shard_map/all_gather | solution.py:126
  164.6 3.8 convolution_convert_fusion.1
  168.5 7.2 %fusion.5 = f32[3,16,128,256]{3,2,1,0:T(8,128)} fusion(bf16[3,16,128,256]{3,1,2,0:T(8,128)(2,1)} %convolution_convert_fusion.1, bf16[3,128,128]{2,0,1:T(4,128)(2,1)S(1)} %fusion.39, bf16[3,256,256]{2,0,1:T(4,128)(2,1)} %fusion.2), kind=kOutput, calls=%fused_computation.8 | convolution fusion | flops 1209532416 | bytes 9928704 | tf_op jit(solution)/shard_map/vzxl,vjl->vzxj/dot_general | solution.py:172
  177.3 8.6 %place.1 = bf16[3,128,16,256]{3,2,1,0:T(8,128)(2,1)S(1)} custom-call(s32[3,128]{1,0:T(4,128)S(1)} %select_reduce_fusion.source, bf16[8,3,16,16,256]{4,3,2,1,0:T(8,128)(2,1)} %copy-done.1, bf16[8,3,16,16,256]{4,3,2,1,0:T(8,128)(2,1)} %bitcast.98), custom_call_target="tpu_custom_call" | custom-call | tf_op jit(solution)/shard_map/place/pallas_call | solution.py:95
  185.9 3.7 fusion
  189.6 5.4 %convert_bitcast_fusion.1 = bf16[3,16,128,256]{2,3,1,0:T(8,128)(2,1)} fusion(bf16[3,16,128,256]{3,2,1,0:T(8,128)(2,1)} %fusion, bf16[3,128,128]{2,0,1:T(4,128)(2,1)S(1)} %fusion.39, bf16[3,256,256]{2,0,1:T(4,128)(2,1)} %fusion.2), kind=kOutput, calls=%fused_computation.18 | convolution fusion | flops 1211105280 | bytes 6782976 | tf_op jit(solution)/shard_map/vik,vziy->vzky/dot_general | solution.py:177
  195.1 4.9 %copy.72 = bf16[3,16,128,256]{3,1,0,2:T(8,128)(2,1)} copy(bf16[3,16,128,256]{2,3,1,0:T(8,128)(2,1)} %convert_bitcast_fusion.1) | data formatting | bytes 6291456 | tf_op jit(solution)/shard_map/convert_element_type | solution.py:179
  200.0 4.6 %convolution_bitcast_fusion.1 = f32[32,128,256]{2,0,1:T(8,128)} fusion(bf16[3,16,128,256]{3,1,0,2:T(8,128)(2,1)} %copy.72, bf16[3,16,32]{2,0,1:T(4,128)(2,1)S(1)} %fusion.46), kind=kOutput, calls=%fused_computation.28 | convolution fusion | flops 100663296 | bytes 7343104 | tf_op jit(solution)/shard_map/vzp,vzxy->pxy/dot_general | solution.py:180
  204.7 41.9 %reduce-scatter.3.cloned.1.call-done = f32[32,32,256]{2,0,1:T(8,128)} async-done(((f32[32,128,256]{2,0,1:T(8,128)}), f32[32,32,256]{2,0,1:T(8,128)}) %reduce-scatter.3.cloned.1.call-update) | async-done | bytes 1048592 | tf_op jit(solution)/shard_map/reduce_scatter | solution.py:183
  247.7 3.4 collective-permute-start.2
  252.4 9.8 %collective-permute-done.2 = f32[8,32,256]{2,0,1:T(8,128)S(1)} collective-permute-done((f32[8,32,256]{2,0,1:T(8,128)S(1)}, f32[8,32,256]{2,0,1:T(8,128)S(1)}, u32[]{:S(2)}, u32[]{:S(2)}) %collective-permute-start.2) | collective-permute-done | bytes 262176 | tf_op jit(solution)/shard_map/ppermute | solution.py:19
  262.2 2.2 fusion.69
  264.4 4.4 %collective-permute-start.4 = (bf16[8,32,256]{2,0,1:T(8,128)(2,1)S(1)}, bf16[8,32,256]{2,0,1:T(8,128)(2,1)S(1)}, u32[]{:S(2)}, u32[]{:S(2)}) collective-permute-start(bf16[8,32,256]{2,0,1:T(8,128)(2,1)S(1)} %get-tuple-element.22), channel_id=1, source_target_pairs={{0,4},{4,8},{8,12},{12,16},{16,20},{20,24},{24,28},{1,5},{5,9},{9,... | collective-permute-start | bytes 393224 | tf_op jit(solution)/shard_map/ppermute | solution.py:19
  271.3 5.2 %collective-permute-done.5 = bf16[8,32,256]{2,0,1:T(8,128)(2,1)S(1)} collective-permute-done((bf16[8,32,256]{2,0,1:T(8,128)(2,1)S(1)}, bf16[8,32,256]{2,0,1:T(8,128)(2,1)S(1)}, u32[]{:S(2)}, u32[]{:S(2)}) %collective-permute-start.5) | collective-permute-done | bytes 131104 | tf_op jit(solution)/shard_map/ppermute | solution.py:19
  277.6 22.7 %all-gather.10.cloned.1.call-done = bf16[32,128,256]{2,0,1:T(8,128)(2,1)} async-done(((bf16[32,32,256]{2,0,1:T(8,128)(2,1)}), bf16[32,128,256]{2,0,1:T(8,128)(2,1)}) %all-gather.10.cloned.1.call-update) | async-done | bytes 2097168 | tf_op jit(solution)/shard_map/all_gather | solution.py:191
  300.3 4.2 convolution_convert_fusion
  304.6 7.2 %fusion.3 = f32[3,16,128,256]{3,2,1,0:T(8,128)} fusion(bf16[3,16,128,256]{3,1,2,0:T(8,128)(2,1)} %convolution_convert_fusion, bf16[3,128,128]{2,0,1:T(4,128)(2,1)S(1)} %fusion.39, bf16[3,256,256]{2,0,1:T(4,128)(2,1)} %fusion.2), kind=kOutput, calls=%fused_computation.6 | convolution fusion | flops 1209532416 | bytes 9928704 | tf_op jit(solution)/shard_map/vzxl,vjl->vzxj/dot_general | solution.py:172
  311.8 6.5 %fusion.1 = bf16[3,16,128,256]{3,2,1,0:T(8,128)(2,1)} fusion(f32[3,16,128,256]{3,2,1,0:T(8,128)} %fusion.3, bf16[3,16,128,256]{3,2,1,0:T(8,128)(2,1)S(1)} %bitcast.97), kind=kLoop, calls=%fused_computation.3 | loop fusion | flops 4718592 | bytes 12582912 | tf_op jit(solution)/shard_map/convert_element_type | solution.py:173
  318.3 5.4 %convert_bitcast_fusion = bf16[3,16,128,256]{2,3,1,0:T(8,128)(2,1)} fusion(bf16[3,16,128,256]{3,2,1,0:T(8,128)(2,1)} %fusion.1, bf16[3,128,128]{2,0,1:T(4,128)(2,1)S(1)} %fusion.39, bf16[3,256,256]{2,0,1:T(4,128)(2,1)} %fusion.2), kind=kOutput, calls=%fused_computation.14 | convolution fusion | flops 1211105280 | bytes 6782976 | tf_op jit(solution)/shard_map/vik,vziy->vzky/dot_general | solution.py:177
  323.7 3.9 copy.76
  327.6 2.7 convolution_bitcast_fusion
  330.4 44.6 %reduce-scatter.5.cloned.1.call-done = f32[32,32,256]{2,0,1:T(8,128)} async-done(((f32[32,128,256]{2,0,1:T(8,128)}), f32[32,32,256]{2,0,1:T(8,128)}) %reduce-scatter.5.cloned.1.call-update) | async-done | bytes 1048592 | tf_op jit(solution)/shard_map/reduce_scatter | solution.py:183
  376.0 3.4 collective-permute-start.6
  380.7 9.8 %collective-permute-done.6 = f32[8,32,256]{2,0,1:T(8,128)S(1)} collective-permute-done((f32[8,32,256]{2,0,1:T(8,128)S(1)}, f32[8,32,256]{2,0,1:T(8,128)S(1)}, u32[]{:S(2)}, u32[]{:S(2)}) %collective-permute-start.6) | collective-permute-done | bytes 262176 | tf_op jit(solution)/shard_map/ppermute | solution.py:19
  392.6 23.8 %all-gather.12.cloned.1.call-done = f32[16,128,256]{2,0,1:T(8,128)} async-done(((f32[16,32,256]{2,0,1:T(8,128)}), f32[16,128,256]{2,0,1:T(8,128)}) %all-gather.12.cloned.1.call-update) | async-done | bytes 2097168 | tf_op jit(solution)/shard_map/all_gather | solution.py:194
  416.3 4.1 copy.77
  (64 shorter events, 22.5 us)
Async XLA Ops:
  6.5 15.4 %copy-start.4 = (s32[3,128]{1,0:T(4,128)S(1)}, s32[3,128]{1,0:T(4,128)}, u32[]{:S(2)}) copy-start(s32[3,128]{1,0:T(4,128)} %param.7) | copy-start | bytes 4612
  6.5 156.8 %all-gather.8.cloned.1.call-start = ((), (), s32[]{:S(2)}) async-start(), calls=%async_computation.3 | async-start | bytes 1310720 | tf_op jit(solution)/shard_map/all_gather | solution.py:160
  9.4 17.8 %copy-start.2 = (f32[16,128,256]{2,0,1:T(8,128)}, f32[16,128,256]{2,0,1:T(8,128)S(1)}, u32[]{:S(2)}) copy-start(f32[16,128,256]{2,0,1:T(8,128)S(1)} %copy.64) | copy-start | bytes 6291460
  9.4 7.6 %collective-permute-start = (bf16[8,32,256]{2,0,1:T(8,128)(2,1)S(1)}, bf16[8,32,256]{2,0,1:T(8,128)(2,1)S(1)}, u32[]{:S(2)}, u32[]{:S(2)}) collective-permute-start(bf16[8,32,256]{2,0,1:T(8,128)(2,1)S(1)} %get-tuple-element.24), channel_id=1, source_target_pairs={{0,4},{4,8},{8,12},{12,16},{16,20},{20,24},{24,28},{1,5},{5,9},{9,... | collective-permute-start | bytes 393224 | tf_op jit(solution)/shard_map/ppermute | solution.py:19
  14.3 6.9 %collective-permute-start.1 = (bf16[8,32,256]{2,0,1:T(8,128)(2,1)S(1)}, bf16[8,32,256]{2,0,1:T(8,128)(2,1)S(1)}, u32[]{:S(2)}, u32[]{:S(2)}) collective-permute-start(bf16[8,32,256]{2,0,1:T(8,128)(2,1)S(1)} %get-tuple-element.25), channel_id=1, source_target_pairs={{4,0},{8,4},{12,8},{16,12},{20,16},{24,20},{28,24},{5,1},{9,5},{13... | collective-permute-start | bytes 393224 | tf_op jit(solution)/shard_map/ppermute | solution.py:19
  27.1 148.5 %all-to-all-start = ((bf16[8,3,16,16,256]{4,3,2,1,0:T(8,128)(2,1)}), bf16[8,3,16,16,256]{4,3,2,1,0:T(8,128)(2,1)S(1)}, u32[]{:S(2)}, u32[]{:S(2)}) async-start(bf16[8,3,16,16,256]{4,3,2,1,0:T(8,128)(2,1)} %get-tuple-element.7), calls=%async_computation | async-start | bytes 6291456 | tf_op jit(solution)/shard_map/all_to_all | solution.py:124
  32.9 4.5 %copy-start.6 = (f32[3,17]{1,0:T(4,128)S(1)}, f32[3,17]{1,0:T(4,128)}, u32[]{:S(2)}) copy-start(f32[3,17]{1,0:T(4,128)} %param.9) | copy-start | bytes 616
  32.9 127.7 %copy-start.5 = (f32[3,2,17]{2,1,0:T(2,128)S(1)}, f32[3,2,17]{2,1,0:T(2,128)}, u32[]{:S(2)}) copy-start(f32[3,2,17]{2,1,0:T(2,128)} %param.8) | copy-start | bytes 1228
  32.9 142.8 %all-gather.14.cloned.1.call-start = ((), (), s32[]{:S(2)}) async-start(), calls=%async_computation.8 | async-start | bytes 3538944 | tf_op jit(solution)/shard_map/all_gather | solution.py:125
  33.7 212.9 %reduce-scatter.3.cloned.1.call-start = ((), (), s32[]{:S(2)}) async-start(), calls=%async_computation.4 | async-start | bytes 5242880 | tf_op jit(solution)/shard_map/reduce_scatter | solution.py:183
  175.6 1.7 copy-start.1
  177.3 8.6 %copy-start = (f32[3,16,128,256]{3,2,1,0:T(8,128)S(1)}, f32[3,16,128,256]{3,2,1,0:T(8,128)}, u32[]{:S(2)}) copy-start(f32[3,16,128,256]{3,2,1,0:T(8,128)} %fusion.5) | copy-start | bytes 18874372
  204.6 95.7 %all-gather.10.cloned.1.call-start = ((), (), s32[]{:S(2)}) async-start(), calls=%async_computation.5 | async-start | bytes 2621440 | tf_op jit(solution)/shard_map/all_gather | solution.py:191
  247.7 14.5 %collective-permute-start.2 = (f32[8,32,256]{2,0,1:T(8,128)S(1)}, f32[8,32,256]{2,0,1:T(8,128)S(1)}, u32[]{:S(2)}, u32[]{:S(2)}) collective-permute-start(f32[8,32,256]{2,0,1:T(8,128)S(1)} %get-tuple-element.18), channel_id=1, source_target_pairs={{0,4},{4,8},{8,12},{12,16},{16,20},{20,24},{24,28},{1,5},{5,9},{9,... | collective-permute-start | bytes 786440 | tf_op jit(solution)/shard_map/ppermute | solution.py:19
  251.1 11.1 %collective-permute-start.3 = (f32[8,32,256]{2,0,1:T(8,128)S(1)}, f32[8,32,256]{2,0,1:T(8,128)S(1)}, u32[]{:S(2)}, u32[]{:S(2)}) collective-permute-start(f32[8,32,256]{2,0,1:T(8,128)S(1)} %get-tuple-element.19), channel_id=1, source_target_pairs={{4,0},{8,4},{12,8},{16,12},{20,16},{24,20},{28,24},{5,1},{9,5},{13... | collective-permute-start | bytes 786440 | tf_op jit(solution)/shard_map/ppermute | solution.py:19
  264.4 6.9 %collective-permute-start.4 = (bf16[8,32,256]{2,0,1:T(8,128)(2,1)S(1)}, bf16[8,32,256]{2,0,1:T(8,128)(2,1)S(1)}, u32[]{:S(2)}, u32[]{:S(2)}) collective-permute-start(bf16[8,32,256]{2,0,1:T(8,128)(2,1)S(1)} %get-tuple-element.22), channel_id=1, source_target_pairs={{0,4},{4,8},{8,12},{12,16},{16,20},{20,24},{24,28},{1,5},{5,9},{9,... | collective-permute-start | bytes 393224 | tf_op jit(solution)/shard_map/ppermute | solution.py:19
  268.8 7.7 %collective-permute-start.5 = (bf16[8,32,256]{2,0,1:T(8,128)(2,1)S(1)}, bf16[8,32,256]{2,0,1:T(8,128)(2,1)S(1)}, u32[]{:S(2)}, u32[]{:S(2)}) collective-permute-start(bf16[8,32,256]{2,0,1:T(8,128)(2,1)S(1)} %get-tuple-element.23), channel_id=1, source_target_pairs={{4,0},{8,4},{12,8},{16,12},{20,16},{24,20},{28,24},{5,1},{9,5},{13... | collective-permute-start | bytes 393224 | tf_op jit(solution)/shard_map/ppermute | solution.py:19
  277.3 97.6 %reduce-scatter.5.cloned.1.call-start = ((), (), s32[]{:S(2)}) async-start(), calls=%async_computation.6 | async-start | bytes 5242880 | tf_op jit(solution)/shard_map/reduce_scatter | solution.py:183
  330.3 60.3 %copy-start.3 = (f32[16,32,256]{2,0,1:T(8,128)S(1)}, f32[16,32,256]{2,0,1:T(8,128)}, u32[]{:S(2)}) copy-start(f32[16,32,256]{2,0,1:T(8,128)} %get-tuple-element.12) | copy-start | bytes 1572868
  330.3 86.0 %all-gather.12.cloned.1.call-start = ((), (), s32[]{:S(2)}) async-start(), calls=%async_computation.7 | async-start | bytes 2621440 | tf_op jit(solution)/shard_map/all_gather | solution.py:194
  376.0 14.6 %collective-permute-start.6 = (f32[8,32,256]{2,0,1:T(8,128)S(1)}, f32[8,32,256]{2,0,1:T(8,128)S(1)}, u32[]{:S(2)}, u32[]{:S(2)}) collective-permute-start(f32[8,32,256]{2,0,1:T(8,128)S(1)} %get-tuple-element.16), channel_id=1, source_target_pairs={{0,4},{4,8},{8,12},{12,16},{16,20},{20,24},{24,28},{1,5},{5,9},{9,... | collective-permute-start | bytes 786440 | tf_op jit(solution)/shard_map/ppermute | solution.py:19
  379.4 11.2 %collective-permute-start.7 = (f32[8,32,256]{2,0,1:T(8,128)S(1)}, f32[8,32,256]{2,0,1:T(8,128)S(1)}, u32[]{:S(2)}, u32[]{:S(2)}) collective-permute-start(f32[8,32,256]{2,0,1:T(8,128)S(1)} %get-tuple-element.17), channel_id=1, source_target_pairs={{4,0},{8,4},{12,8},{16,12},{20,16},{24,20},{28,24},{5,1},{9,5},{13... | collective-permute-start | bytes 786440 | tf_op jit(solution)/shard_map/ppermute | solution.py:19
Sparse Core Ops, SparseCore 0:
  22.0 17.9 all-gather.7
  42.2 99.2 all-gather.13
  204.7 41.8 reduce-scatter.2
  277.5 22.8 all-gather.9
  330.4 44.4 reduce-scatter.4
  392.7 23.5 all-gather.11

commit v2 on v1

--- a/solution.py
+++ b/solution.py
@@ -1,3 +1,5 @@
+import functools
+
 import jax
 import jax.numpy as jnp
 from jax import lax
@@ -116,6 +118,8 @@
     slabs = lax.axis_size("gz")
     group = blk_num // slabs
     me = lax.axis_index("gz")
+    dests = lax.all_gather(block_dest, "gz", axis=0)
+    dests, block_dest = lax.optimization_barrier((dests, block_dest))
     target, placed, rank = slots_of(block_dest, blk_num, slabs)
     slot = jnp.where(rank < group, target * group + rank, slabs * group + rank - group)
     hit = slot[:, None, :] == jnp.arange((slabs + 1) * group)[None, :, None]
@@ -123,7 +127,6 @@
     packed, extra = pack(source, raw_views, slabs, group)
     main = lax.all_to_all(packed, "gz", split_axis=0, concat_axis=0, tiled=True)
     late = lax.all_gather(extra, "gz", axis=0)
-    dests = lax.all_gather(block_dest, "gz", axis=0)
     target, placed, rank = slots_of(dests, blk_num, slabs)
     slab_ids = jnp.arange(slabs)[:, None, None]
     code = slab_ids * 65536 + jnp.where(rank < group, rank, 256 + rank - group)
@@ -136,11 +139,226 @@
     return place(inverse, main, late)
 
 
-def with_halo(quarter, radius):
+def exchange_kernel(last, partial, held, *refs):
+    if last:
+        (result, got_a, forward, got_b, edge, got_halo, send_sem, recv_sem) = refs
+    else:
+        (renewed, result, got_a, forward, got_b, edge, got_halo, send_sem, recv_sem) = refs
+    planes, rows_q, _ = held.shape
+    radius = edge.shape[1]
+    half = planes // 2
+    slab, slabs = lax.axis_index("gz"), lax.axis_size("gz")
+    part, parts = lax.axis_index("vert"), lax.axis_size("vert")
+    near = part + 1 - 2 * (part % 2)
+    far = (part + 2) % parts
+    near_far = (near + 2) % parts
+    has_below, has_above = slab > 0, slab < slabs - 1
+    taken = [0]
+
+    def rows(quarter):
+        return pl.ds(pl.multiple_of(quarter * rows_q, rows_q), rows_q)
+
+    def remote(source, target, device):
+        place = taken[0]
+        taken[0] += 1
+        return pltpu.make_async_remote_copy(
+            src_ref=source,
+            dst_ref=target,
+            send_sem=send_sem.at[place],
+            recv_sem=recv_sem.at[place],
+            device_id=device,
+            device_id_type=pl.DeviceIdType.MESH,
+        )
+
+    barrier = pltpu.get_barrier_semaphore()
+
+    def greet(device):
+        pl.semaphore_signal(barrier, inc=1, device_id=device, device_id_type=pl.DeviceIdType.MESH)
+
+    greet({"vert": near})
+    greet({"vert": far})
+    pl.when(has_below)(lambda: greet({"gz": slab - 1}))
+    pl.when(has_above)(lambda: greet({"gz": slab + 1}))
+    pl.semaphore_wait(barrier, 2 + jnp.minimum(slab, 1) + jnp.minimum(slabs - 1 - slab, 1))
+
+    chunks = [
+        pl.ds(0, radius),
+        pl.ds(planes + radius, radius),
+        pl.ds(radius, half),
+        pl.ds(radius + half, half),
+    ]
+    waits = []
+    stage_a = []
+    for chunk in chunks:
+        passing = remote(partial.at[chunk, rows(near_far)], got_a.at[1, chunk], {"vert": near})
+        passing.start()
+        staying = remote(partial.at[chunk, rows(near)], got_a.at[0, chunk], {"vert": near})
+        staying.start()
+        stage_a.append((passing, staying))
+        waits += [passing, staying]
+
+    @pl.when(jnp.logical_not(has_below))
+    def _():
+        got_halo[0] = jnp.zeros(got_halo.shape[1:], got_halo.dtype)
+
+    @pl.when(jnp.logical_not(has_above))
+    def _():
+        got_halo[1] = jnp.zeros(got_halo.shape[1:], got_halo.dtype)
+
+    if not last:
+
+        @pl.when(jnp.logical_not(has_below))
+        def _():
+            result[pl.ds(0, radius), rows(part)] = jnp.zeros(
+                (radius, rows_q, result.shape[2]), result.dtype
+            )
+
+        @pl.when(jnp.logical_not(has_above))
+        def _():
+            result[pl.ds(planes + radius, radius), rows(part)] = jnp.zeros(
+                (radius, rows_q, result.shape[2]), result.dtype
+            )
+
+    stage_b = []
+    for chunk, (passing, _) in zip(chunks, stage_a):
+        passing.wait_recv()
+        forward[chunk] = partial[chunk, rows(far)] + got_a[1, chunk]
+        copy = remote(forward.at[chunk], got_b.at[chunk], {"vert": far})
+        copy.start()
+        stage_b.append(copy)
+        waits.append(copy)
+
+    def total(place):
+        chunk = chunks[place]
+        stage_a[place][1].wait_recv()
+        stage_b[place].wait_recv()
+        return (partial[chunk, rows(part)] + got_a[0, chunk]) + got_b[chunk]
+
+    edge[0] = total(0)
+    down = remote(edge.at[0], got_halo.at[1], {"gz": slab - 1})
+    pl.when(has_below)(lambda: down.start())
+    edge[1] = total(1)
+    up = remote(edge.at[1], got_halo.at[0], {"gz": slab + 1})
+    pl.when(has_above)(lambda: up.start())
+
+    inner = 0 if last else radius
+    shared = []
+    besides = []
+    moved = []
+    for place in range(2):
+        summed = total(2 + place)
+        if place == 0:
+            pl.when(has_below)(lambda: up.wait_recv())
+        else:
+            pl.when(has_above)(lambda: down.wait_recv())
+        own = pl.ds(place * half, half)
+        value = held[own] * (summed + got_halo[place]) / VIEWS
+        if not last:
+            renewed[own] = value
+        target = result.at[pl.ds(inner + place * half, half), rows(part)]
+        target[...] = value.astype(result.dtype)
+        if not last:
+            if place == 0:
+                copy = remote(
+                    target, result.at[pl.ds(planes + radius, radius), rows(part)], {"gz": slab - 1}
+                )
+                pl.when(has_below)(functools.partial(copy.start))
+            else:
+                copy = remote(target, result.at[pl.ds(0, radius), rows(part)], {"gz": slab + 1})
+                pl.when(has_above)(functools.partial(copy.start))
+            moved.append(copy)
+        across = remote(target, target, {"vert": far})
+        across.start()
+        beside = remote(target, target, {"vert": near})
+        beside.start()
+        shared.append((inner + place * half, half, across))
+        waits += [across, beside]
+        besides.append(beside)
+    late = []
+
+    def relay(start, length, across):
+        across.wait_recv()
+        target = result.at[pl.ds(start, length), rows(far)]
+        copy = remote(target, target, {"vert": near})
+        copy.start()
+        late.append(copy)
+
+    if last:
+        for item in shared:
+            relay(*item)
+    else:
+        relay(*shared[0])
+        relay(*shared[1])
+        outer = []
+        for place in range(2):
+            start = planes + radius if place == 0 else 0
+            pl.when(has_above if place == 0 else has_below)(
+                functools.partial(moved[place].wait_recv)
+            )
+            target = result.at[pl.ds(start, radius), rows(part)]
+            across = remote(target, target, {"vert": far})
+            across.start()
+            beside = remote(target, target, {"vert": near})
+            beside.start()
+            outer.append((start, radius, across))
+            late.append(beside)
+        for item in outer:
+            relay(*item)
+            waits.append(item[2])
+        pl.when(has_below)(lambda: moved[0].wait_send())
+        pl.when(has_above)(lambda: moved[1].wait_send())
+    pl.when(has_below)(lambda: down.wait_send())
+    pl.when(has_above)(lambda: up.wait_send())
+    for copy in waits:
+        copy.wait_send()
+    for copy in late:
+        copy.wait_send()
+        copy.wait_recv()
+    for copy in besides:
+        copy.wait_recv()
+
+
+def exchange(partial, held, last):
+    whole, rows_x, rows_y = partial.shape
+    planes, rows_q, _ = held.shape
+    radius = (whole - planes) // 2
+    assert planes == 2 * radius and rows_x == 4 * rows_q
+    vmem = pl.BlockSpec(memory_space=pltpu.VMEM)
+    f32 = jnp.float32
+    if last:
+        out_shape = jax.ShapeDtypeStruct((planes, rows_x, rows_y), f32)
+        out_specs = vmem
+    else:
+        out_shape = (
+            jax.ShapeDtypeStruct(held.shape, f32),
+            jax.ShapeDtypeStruct((whole, rows_x, rows_y), jnp.bfloat16),
+        )
+        out_specs = (vmem, vmem)
+    copies = 20 if last else 28
+    return pl.pallas_call(
+        functools.partial(exchange_kernel, last),
+        out_shape=out_shape,
+        in_specs=[vmem, vmem],
+        out_specs=out_specs,
+        scratch_shapes=[
+            pltpu.VMEM((2, whole, rows_q, rows_y), f32),
+            pltpu.VMEM((whole, rows_q, rows_y), f32),
+            pltpu.VMEM((whole, rows_q, rows_y), f32),
+            pltpu.VMEM((2, radius, rows_q, rows_y), f32),
+            pltpu.VMEM((2, radius, rows_q, rows_y), f32),
+            pltpu.SemaphoreType.DMA((copies,)),
+            pltpu.SemaphoreType.DMA((copies,)),
+        ],
+        compiler_params=pltpu.CompilerParams(
+            collective_id=1 if last else 0, has_side_effects=True, vmem_limit_bytes=VMEM_LIMIT
+        ),
+        name="finish" if last else "renew",
+    )(partial, held)
+
+
+def halo_of(quarter, radius):
     planes = quarter.shape[0]
-    before = shift(quarter[planes - radius:], "gz", 1)
-    after = shift(quarter[:radius], "gz", -1)
-    return before, after
+    return shift(quarter[planes - radius:], "gz", 1), shift(quarter[:radius], "gz", -1)
 
 
 def body(estimate, raw_views, block_dest, lateral_psf, axial_psf):
@@ -156,7 +374,7 @@
     rows_q = rows_x // parts
     mine = lax.axis_index("vert") * rows_q
     held = lax.dynamic_slice_in_dim(estimate, mine, rows_q, axis=1)
-    before, after = with_halo(held.astype(jnp.bfloat16), radius)
+    before, after = halo_of(held.astype(jnp.bfloat16), radius)
     sides = lax.all_gather(jnp.concatenate([before, after], axis=0), "vert", axis=1, tiled=True)
     widened = jnp.concatenate(
         [sides[:radius], estimate.astype(jnp.bfloat16), sides[radius:]], axis=0
@@ -180,18 +398,11 @@
         partial_back = jnp.einsum(
             "vzp,vzxy->pxy", front_matrix, fourth, preferred_element_type=jnp.float32
         )
-        summed = lax.psum_scatter(partial_back, "vert", scatter_dimension=1, tiled=True)
-        below = shift(summed[planes + radius:], "gz", 1)
-        above = shift(summed[:radius], "gz", -1)
-        correction = summed[radius:planes + radius] + jnp.concatenate([below, above], axis=0)
-        held = held * correction / VIEWS
         if iteration < ITERS - 1:
-            lowered = held.astype(jnp.bfloat16)
-            before, after = with_halo(lowered, radius)
-            widened = lax.all_gather(
-                jnp.concatenate([before, lowered, after], axis=0), "vert", axis=1, tiled=True
-            )
-    return lax.all_gather(held, "vert", axis=1, tiled=True)
+            held, widened = exchange(partial_back, held, False)
+        else:
+            held = exchange(partial_back, held, True)
+    return held
 
 
 def solution(mesh):

time: 428 us -> 319 us (0.75)
  blocking collectives: 122 us -> 27 us
  Pallas kernels: 13.3 us -> 98.3 us
  waiting for transfers between devices: 165 us -> 89.5 us
  starting transfers between devices: 27.4 us -> 9.84 us
  matrix products: 43.3 us -> 36.9 us
    all_gather x1, blocking collectives: 122 us -> 27 us  [route(): dests = lax.all_gather(block_dest, 'gz', axis=0)]
    reduce_scatter x2 -> x0, waiting for transfers between devices: 86.5 us -> none  [body(): lax.psum_scatter(partial_back, 'vert', scatter_dimension=1, tiled=True)]
    pallas_call x0 -> x2, Pallas kernels: none -> 85 us  [exchange(): pl.pallas_call(functools.partial(exchange_kernel, last), out_shape=out_sh...]
    all_to_all x1, waiting for transfers between devices: 0.01 us -> 83.2 us  [route(): main = lax.all_to_all(packed, 'gz', split_axis=0, concat_axis=0, tiled=True)]
    all_gather x2 -> x0, waiting for transfers between devices: 46.5 us -> none  [the longest x1 23.8 us: body(): return lax.all_gather(held, 'vert', axis=1, tiled=True)]
    ppermute x8 -> x2, waiting for transfers between devices: 31.6 us -> 5.56 us  [shift(): return lax.ppermute(array, axis, pairs)]
    ppermute x8 -> x2, starting transfers between devices: 21.2 us -> 6.14 us  [shift(): return lax.ppermute(array, axis, pairs)]
    dot_general x0 -> x2, local copies, waits for them, and re-layouts: none -> 8.73 us  [body(): jnp.einsum('vzp,vzxy->pxy', front_matrix, fourth, preferred_element_type=...]
  transfers between devices with their start and end apart: 15 -> 5, of which waited for: 10 -> 3; matrix products, arithmetic and copies ran while one was open for 5% -> 7% of each run, Pallas kernels for 1% -> 1%
where the time goes in v2:
time: 319 us
  Pallas kernels  98.3 us (31%)
  waiting for transfers between devices  89.5 us (28%)
  matrix products  36.9 us (12%)
  blocking collectives  27 us (8%)
  local copies, waits for them, and re-layouts  26.9 us (8%)
  other arithmetic  16.5 us (5%)
  between operations  13.6 us (4%)
  starting transfers between devices  9.84 us (3%)
    pallas_call x2, Pallas kernels, exchange(): pl.pallas_call(functools.partial(exchange_kernel, last), out_shape=out_sh...  85 us
    all_to_all x1, waiting for transfers between devices, route(): main = lax.all_to_all(packed, 'gz', split_axis=0, concat_axis=0, tiled=True)  83.2 us
    all_gather x1, blocking collectives, route(): dests = lax.all_gather(block_dest, 'gz', axis=0)  27 us
    dot_general x2, matrix products, body(): jnp.einsum('vzxl,vjl->vzxj', second, mat_y, preferred_element_type=jnp.fl...  14.3 us
    dot_general x2, matrix products, body(): jnp.einsum('vik,vziy->vzky', mat_x, third, preferred_element_type=jnp.flo...  10.9 us
    convert_element_type x2, other arithmetic, body(): ratio = (observed.astype(jnp.float32) / blurred).astype(jnp.bfloat16)  10.2 us
    convert_element_type x2, local copies, waits for them, and re-layouts, body(): fourth = jnp.einsum('vik,vziy->vzky', mat_x, third, preferred_element_typ...  8.79 us
    dot_general x2, local copies, waits for them, and re-layouts, body(): jnp.einsum('vzp,vzxy->pxy', front_matrix, fourth, preferred_element_type=...  8.73 us
  transfers between devices with their start and end apart: 5, of which 3 were waited for; matrix products, arithmetic and copies ran while one was open for 7% of the time, Pallas kernels for 1%

profile of v2, /device:TPU:0, one launch (start us, length us, event | category | flops | bytes accessed | tf_op | source)
XLA Modules:
  0.0 318.6 jit_solution(4622668883527906566)
XLA Ops:
  6.5 1.9 fusion.66
  8.5 4.8 %collective-permute-start = (bf16[8,32,256]{2,1,0:T(8,128)(2,1)S(1)}, bf16[8,32,256]{2,1,0:T(8,128)(2,1)S(1)}, u32[]{:S(2)}, u32[]{:S(2)}) collective-permute-start(bf16[8,32,256]{2,1,0:T(8,128)(2,1)S(1)} %get-tuple-element.26), channel_id=1, source_target_pairs={{0,4},{4,8},{8,12},{12,16},{16,20},{20,24},{24,28},{1,5},{5,9},{9,... | collective-permute-start | bytes 393224 | tf_op jit(solution)/shard_map/ppermute | solution.py:21
  13.3 1.3 collective-permute-start.1
  14.6 1.4 collective-permute-done
  16.1 4.1 %collective-permute-done.1 = bf16[8,32,256]{2,1,0:T(8,128)(2,1)S(1)} collective-permute-done((bf16[8,32,256]{2,1,0:T(8,128)(2,1)S(1)}, bf16[8,32,256]{2,1,0:T(8,128)(2,1)S(1)}, u32[]{:S(2)}, u32[]{:S(2)}) %collective-permute-start.1) | collective-permute-done | bytes 131104 | tf_op jit(solution)/shard_map/ppermute | solution.py:21
  21.0 27.0 %all-gather.2 = s32[8,3,128]{2,1,0:T(4,128)S(1)} all-gather(s32[1,3,128]{2,1,0:T(4,128)} %bitcast.99), channel_id=2, replica_groups=mesh['gz'=8,'vert'=4] {'gz'}, dimensions={0}, use_global_device_ids=true | all-gather | bytes 13824 | tf_op jit(solution)/shard_map/all_gather | solution.py:121
  49.8 4.7 %pack.1 = (bf16[8,3,16,16,256]{4,3,2,1,0:T(8,128)(2,1)}, bf16[3,16,16,256]{3,2,1,0:T(8,128)(2,1)}) custom-call(s32[3,144]{1,0:T(4,128)S(1)} %select_reduce_fusion.1.source, bf16[3,128,16,256]{3,2,1,0:T(8,128)(2,1)} %raw.1), custom_call_target="tpu_custom_call" | custom-call | tf_op jit(solution)/shard_map/pack/pallas_call | solution.py:62
  54.5 3.6 %all-to-all-start = ((bf16[8,3,16,16,256]{4,3,2,1,0:T(8,128)(2,1)}), bf16[8,3,16,16,256]{4,3,2,1,0:T(8,128)(2,1)S(1)}, u32[]{:S(2)}, u32[]{:S(2)}) async-start(bf16[8,3,16,16,256]{4,3,2,1,0:T(8,128)(2,1)} %get-tuple-element.13), calls=%async_computation | async-start | bytes 6291456 | tf_op jit(solution)/shard_map/all_to_all | solution.py:128
  59.0 3.7 %copy.130 = bf16[16,128,256]{2,0,1:T(8,128)(2,1)} copy(f32[16,128,256]{2,1,0:T(8,128)} %param.5) | data formatting | bytes 3145728 | tf_op args[0]
  62.9 1.2 convert_reduce_fusion
  65.1 2.1 fusion.2
  67.2 1.4 fusion.67
  69.2 2.6 convolution_convert_fusion.1
  71.8 7.2 %fusion.5 = f32[3,16,128,256]{3,2,1,0:T(8,128)} fusion(bf16[3,16,128,256]{3,1,2,0:T(8,128)(2,1)} %convolution_convert_fusion.1, bf16[3,128,128]{2,0,1:T(4,128)(2,1)S(1)} %fusion.40, bf16[3,256,256]{2,0,1:T(4,128)(2,1)} %fusion.2), kind=kOutput, calls=%fused_computation.8 | convolution fusion | flops 1209532416 | bytes 9928704 | tf_op jit(solution)/shard_map/vzxl,vjl->vzxj/dot_general | solution.py:390
  78.9 83.2 %all-to-all-done.main = bf16[8,3,16,16,256]{4,3,2,1,0:T(8,128)(2,1)S(1)} async-done(((bf16[8,3,16,16,256]{4,3,2,1,0:T(8,128)(2,1)}), bf16[8,3,16,16,256]{4,3,2,1,0:T(8,128)(2,1)S(1)}, u32[]{:S(2)}, u32[]{:S(2)}) %all-to-all-start) | async-done | bytes 3145760 | tf_op jit(solution)/shard_map/all_to_all | solution.py:128
  162.1 1.6 copy-done.4
  163.8 8.6 %place.1 = bf16[3,128,16,256]{3,2,1,0:T(8,128)(2,1)S(1)} custom-call(s32[3,128]{1,0:T(4,128)S(1)} %select_reduce_fusion.source, bf16[8,3,16,16,256]{4,3,2,1,0:T(8,128)(2,1)} %copy-done.4, bf16[8,3,16,16,256]{4,3,2,1,0:T(8,128)(2,1)} %bitcast.98), custom_call_target="tpu_custom_call" | custom-call | tf_op jit(solution)/shard_map/place/pallas_call | solution.py:97
  172.4 3.7 %fusion = bf16[3,16,128,256]{3,2,1,0:T(8,128)(2,1)} fusion(f32[3,16,128,256]{3,2,1,0:T(8,128)S(1)} %copy-done.3, bf16[3,16,128,256]{3,2,1,0:T(8,128)(2,1)S(1)} %bitcast.96), kind=kLoop, calls=%fused_computation.2 | loop fusion | flops 4718592 | bytes 12582912 | tf_op jit(solution)/shard_map/convert_element_type | solution.py:391
  176.1 5.4 %convert_bitcast_fusion.1 = bf16[3,16,128,256]{2,3,1,0:T(8,128)(2,1)} fusion(bf16[3,16,128,256]{3,2,1,0:T(8,128)(2,1)} %fusion, bf16[3,128,128]{2,0,1:T(4,128)(2,1)S(1)} %fusion.40, bf16[3,256,256]{2,0,1:T(4,128)(2,1)} %fusion.2), kind=kOutput, calls=%fused_computation.18 | convolution fusion | flops 1211105280 | bytes 6782976 | tf_op jit(solution)/shard_map/vik,vziy->vzky/dot_general | solution.py:395
  181.5 4.9 %copy.75 = bf16[3,16,128,256]{3,1,0,2:T(8,128)(2,1)} copy(bf16[3,16,128,256]{2,3,1,0:T(8,128)(2,1)} %convert_bitcast_fusion.1) | data formatting | bytes 6291456 | tf_op jit(solution)/shard_map/convert_element_type | solution.py:397
  186.4 2.6 convolution_bitcast_fusion.1
  189.1 4.4 %copy.76.partial = f32[32,128,256]{2,1,0:T(8,128)} copy(f32[32,128,256]{2,0,1:T(8,128)S(1)} %convolution_bitcast_fusion.1) | data formatting | bytes 8388608 | tf_op jit(solution)/shard_map/vzp,vzxy->pxy/dot_general | solution.py:398
  193.4 43.1 %renew.1 = (f32[16,32,256]{2,1,0:T(8,128)S(1)}, bf16[32,128,256]{2,1,0:T(8,128)(2,1)S(1)}) custom-call(f32[32,128,256]{2,1,0:T(8,128)} %copy.76.partial, f32[16,32,256]{2,1,0:T(8,128)S(1)} %copy-done), custom_call_target="tpu_custom_call" | custom-call | tf_op jit(solution)/shard_map/renew/pallas_call | solution.py:338
  236.6 0.8 copy-done.1
  237.4 3.1 convolution_convert_fusion
  240.5 7.2 %fusion.3 = f32[3,16,128,256]{3,2,1,0:T(8,128)} fusion(bf16[3,16,128,256]{3,1,2,0:T(8,128)(2,1)} %convolution_convert_fusion, bf16[3,128,128]{2,0,1:T(4,128)(2,1)S(1)} %fusion.40, bf16[3,256,256]{2,0,1:T(4,128)(2,1)} %fusion.2), kind=kOutput, calls=%fused_computation.6 | convolution fusion | flops 1209532416 | bytes 9928704 | tf_op jit(solution)/shard_map/vzxl,vjl->vzxj/dot_general | solution.py:390
  247.6 6.5 %fusion.1 = bf16[3,16,128,256]{3,2,1,0:T(8,128)(2,1)} fusion(f32[3,16,128,256]{3,2,1,0:T(8,128)} %fusion.3, bf16[3,16,128,256]{3,2,1,0:T(8,128)(2,1)S(1)} %bitcast.97), kind=kLoop, calls=%fused_computation.3 | loop fusion | flops 4718592 | bytes 12582912 | tf_op jit(solution)/shard_map/convert_element_type | solution.py:391
  254.1 5.4 %convert_bitcast_fusion = bf16[3,16,128,256]{2,3,1,0:T(8,128)(2,1)} fusion(bf16[3,16,128,256]{3,2,1,0:T(8,128)(2,1)} %fusion.1, bf16[3,128,128]{2,0,1:T(4,128)(2,1)S(1)} %fusion.40, bf16[3,256,256]{2,0,1:T(4,128)(2,1)} %fusion.2), kind=kOutput, calls=%fused_computation.14 | convolution fusion | flops 1211105280 | bytes 6782976 | tf_op jit(solution)/shard_map/vik,vziy->vzky/dot_general | solution.py:395
  259.6 3.9 %copy.81 = bf16[3,16,128,256]{3,1,0,2:T(8,128)(2,1)S(1)} copy(bf16[3,16,128,256]{2,3,1,0:T(8,128)(2,1)} %convert_bitcast_fusion) | data formatting | bytes 6291456 | tf_op jit(solution)/shard_map/convert_element_type | solution.py:397
  264.2 4.4 %copy.82.partial = f32[32,128,256]{2,1,0:T(8,128)} copy(f32[32,128,256]{2,0,1:T(8,128)S(1)} %convolution_bitcast_fusion) | data formatting | bytes 8388608 | tf_op jit(solution)/shard_map/vzp,vzxy->pxy/dot_general | solution.py:398
  268.6 41.9 %finish.1 = f32[16,128,256]{2,1,0:T(8,128)S(1)} custom-call(f32[32,128,256]{2,1,0:T(8,128)} %copy.82.partial, f32[16,32,256]{2,1,0:T(8,128)S(1)} %copy-done.2), custom_call_target="tpu_custom_call" | custom-call | tf_op jit(solution)/shard_map/finish/pallas_call | solution.py:338
  310.5 1.3 copy.161
  (41 shorter events, 5.9 us)
Async XLA Ops:
  6.5 60.6 %all-gather.6.cloned.1.call-start = ((), (), s32[]{:S(2)}) async-start(), calls=%async_computation.1 | async-start | bytes 1310720 | tf_op jit(solution)/shard_map/all_gather | solution.py:378
  8.5 7.6 %collective-permute-start = (bf16[8,32,256]{2,1,0:T(8,128)(2,1)S(1)}, bf16[8,32,256]{2,1,0:T(8,128)(2,1)S(1)}, u32[]{:S(2)}, u32[]{:S(2)}) collective-permute-start(bf16[8,32,256]{2,1,0:T(8,128)(2,1)S(1)} %get-tuple-element.26), channel_id=1, source_target_pairs={{0,4},{4,8},{8,12},{12,16},{16,20},{20,24},{24,28},{1,5},{5,9},{9,... | collective-permute-start | bytes 393224 | tf_op jit(solution)/shard_map/ppermute | solution.py:21
  13.3 6.9 %collective-permute-start.1 = (bf16[8,32,256]{2,1,0:T(8,128)(2,1)S(1)}, bf16[8,32,256]{2,1,0:T(8,128)(2,1)S(1)}, u32[]{:S(2)}, u32[]{:S(2)}) collective-permute-start(bf16[8,32,256]{2,1,0:T(8,128)(2,1)S(1)} %get-tuple-element.27), channel_id=1, source_target_pairs={{4,0},{8,4},{12,8},{16,12},{20,16},{24,20},{28,24},{5,1},{9,5},{13... | collective-permute-start | bytes 393224 | tf_op jit(solution)/shard_map/ppermute | solution.py:21
  54.5 107.6 %all-to-all-start = ((bf16[8,3,16,16,256]{4,3,2,1,0:T(8,128)(2,1)}), bf16[8,3,16,16,256]{4,3,2,1,0:T(8,128)(2,1)S(1)}, u32[]{:S(2)}, u32[]{:S(2)}) async-start(bf16[8,3,16,16,256]{4,3,2,1,0:T(8,128)(2,1)} %get-tuple-element.13), calls=%async_computation | async-start | bytes 6291456 | tf_op jit(solution)/shard_map/all_to_all | solution.py:128
  58.2 4.5 %copy-start.7 = (f32[3,17]{1,0:T(4,128)S(1)}, f32[3,17]{1,0:T(4,128)}, u32[]{:S(2)}) copy-start(f32[3,17]{1,0:T(4,128)} %param.9) | copy-start | bytes 616
  58.2 6.2 %copy-start.6 = (f32[3,2,17]{2,1,0:T(2,128)S(1)}, f32[3,2,17]{2,1,0:T(2,128)}, u32[]{:S(2)}) copy-start(f32[3,2,17]{2,1,0:T(2,128)} %param.8) | copy-start | bytes 1228
  58.2 103.9 %all-gather.8.cloned.1.call-start = ((), (), s32[]{:S(2)}) async-start(), calls=%async_computation.2 | async-start | bytes 3538944 | tf_op jit(solution)/shard_map/all_gather | solution.py:129
  67.2 2.0 copy-start.5
  162.1 1.6 copy-start.4
  163.8 8.6 %copy-start.3 = (f32[3,16,128,256]{3,2,1,0:T(8,128)S(1)}, f32[3,16,128,256]{3,2,1,0:T(8,128)}, u32[]{:S(2)}) copy-start(f32[3,16,128,256]{3,2,1,0:T(8,128)} %fusion.5) | copy-start | bytes 18874372
  189.1 4.4 %copy-start = (f32[16,32,256]{2,1,0:T(8,128)S(1)}, f32[16,32,256]{2,1,0:T(8,128)}, u32[]{:S(2)}) copy-start(f32[16,32,256]{2,1,0:T(8,128)} %get-tuple-element.23.held) | copy-start | bytes 1572868
  236.6 0.8 copy-start.1
  264.2 4.4 %copy-start.2 = (f32[16,32,256]{2,1,0:T(8,128)S(1)}, f32[16,32,256]{2,1,0:T(8,128)}, u32[]{:S(2)}) copy-start(f32[16,32,256]{2,1,0:T(8,128)} %copy-done.1) | copy-start | bytes 1572868
Sparse Core Ops, SparseCore 0:
  21.1 17.9 all-gather.5
  61.2 100.7 all-gather.7

commit v3 on v2

--- a/solution.py
+++ b/solution.py
@@ -10,15 +10,6 @@
 VIEWS = 12
 ITERS = 2
 VMEM_LIMIT = 48 * 1024 * 1024
-
-
-def shift(array, axis, step):
-    count = lax.axis_size(axis)
-    if step > 0:
-        pairs = [(i, i + 1) for i in range(count - 1)]
-    else:
-        pairs = [(i + 1, i) for i in range(count - 1)]
-    return lax.ppermute(array, axis, pairs)
 
 
 def normalize(kernel):
@@ -72,6 +63,203 @@
     )(source, raw)
 
 
+def spread_kernel(estimate, extra, dest, widened, late, dests, send_sem, recv_sem):
+    planes, rows_x, rows_y = estimate.shape
+    radius = (widened.shape[0] - planes) // 2
+    slab, slabs = lax.axis_index("gz"), lax.axis_size("gz")
+    part, parts = lax.axis_index("vert"), lax.axis_size("vert")
+    rows_q = rows_x // parts
+    near = part + 1 - 2 * (part % 2)
+    far = (part + 2) % parts
+    lines = slabs // 2
+    line, side = slab // 2, slab % 2
+    other = slab + 1 - 2 * side
+    has_below, has_above = slab > 0, slab < slabs - 1
+    line_below, line_above = line > 0, line < lines - 1
+    taken = [0]
+
+    def rows(quarter):
+        return pl.ds(pl.multiple_of(quarter * rows_q, rows_q), rows_q)
+
+    def remote(source, target, device):
+        place = taken[0]
+        taken[0] += 1
+        return pltpu.make_async_remote_copy(
+            src_ref=source,
+            dst_ref=target,
+            send_sem=send_sem.at[place],
+            recv_sem=recv_sem.at[place],
+            device_id=device,
+            device_id_type=pl.DeviceIdType.MESH,
+        )
+
+    def groups(index, device):
+        return (
+            remote(late.at[index], late.at[index], device),
+            remote(dests.at[index], dests.at[index], device),
+        )
+
+    def start(copies):
+        for copy in copies:
+            copy.start()
+
+    def wait_recv(copies):
+        for copy in copies:
+            copy.wait_recv()
+
+    def wait_send(copies):
+        for copy in copies:
+            copy.wait_send()
+
+    barrier = pltpu.get_barrier_semaphore()
+
+    def greet(device):
+        pl.semaphore_signal(barrier, inc=1, device_id=device, device_id_type=pl.DeviceIdType.MESH)
+
+    greet({"vert": near})
+    greet({"vert": far})
+    pl.when(has_below)(lambda: greet({"gz": slab - 1}))
+    pl.when(has_above)(lambda: greet({"gz": slab + 1}))
+    pl.when(line_below)(lambda: greet({"gz": slab - 2}))
+    pl.when(line_above)(lambda: greet({"gz": slab + 2}))
+    pl.semaphore_wait(
+        barrier,
+        2
+        + jnp.minimum(slab, 1)
+        + jnp.minimum(slabs - 1 - slab, 1)
+        + jnp.minimum(line, 1)
+        + jnp.minimum(lines - 1 - line, 1),
+    )
+
+    for edge in (0, planes - radius):
+        widened[pl.ds(radius + edge, radius), rows(part)] = estimate[
+            pl.ds(edge, radius), rows(part)
+        ].astype(widened.dtype)
+    lowest = widened.at[pl.ds(radius, radius), rows(part)]
+    highest = widened.at[pl.ds(planes, radius), rows(part)]
+    before = widened.at[pl.ds(0, radius), rows(part)]
+    after = widened.at[pl.ds(planes + radius, radius), rows(part)]
+    down = remote(lowest, after, {"gz": slab - 1})
+    up = remote(highest, before, {"gz": slab + 1})
+    pl.when(has_below)(down.start)
+    pl.when(has_above)(up.start)
+
+    late[slab] = extra[...]
+    dests[slab] = dest[...]
+    swaps = [(None, groups(slab, {"gz": other}))]
+    rising, falling = [], []
+    for step in range(lines - 1):
+        index = jnp.maximum(line - step, 0) * 2 + side
+        rising.append((line_above & (line >= step), groups(index, {"gz": slab + 2})))
+        index = jnp.minimum(line + step, lines - 1) * 2 + side
+        falling.append((line_below & (line + step < lines), groups(index, {"gz": slab - 2})))
+    pl.when(rising[0][0])(lambda: start(rising[0][1]))
+    pl.when(falling[0][0])(lambda: start(falling[0][1]))
+    start(swaps[0][1])
+
+    @pl.when(jnp.logical_not(has_below))
+    def _():
+        before[...] = jnp.zeros(before.shape, before.dtype)
+
+    @pl.when(jnp.logical_not(has_above))
+    def _():
+        after[...] = jnp.zeros(after.shape, after.dtype)
+
+    half = rows_x // parts
+    for quarter in range(parts):
+        own = pl.ds(quarter * half, half)
+
+        @pl.when(part != quarter)
+        def _():
+            widened[pl.ds(radius, planes), own] = estimate[:, own].astype(widened.dtype)
+
+    middle = planes - 2 * radius
+    if middle:
+        widened[pl.ds(2 * radius, middle), rows(part)] = estimate[
+            pl.ds(radius, middle), rows(part)
+        ].astype(widened.dtype)
+
+    sides = []
+    for start_plane, landed, copy, exists in (
+        (0, before, up, has_below),
+        (planes + radius, after, down, has_above),
+    ):
+        pl.when(exists)(copy.wait_recv)
+        across = remote(landed, landed, {"vert": far})
+        across.start()
+        beside = remote(landed, landed, {"vert": near})
+        beside.start()
+        sides.append((start_plane, across, beside))
+    relays = []
+    for start_plane, across, beside in sides:
+        across.wait_recv()
+        landed = widened.at[pl.ds(start_plane, radius), rows(far)]
+        copy = remote(landed, landed, {"vert": near})
+        copy.start()
+        relays.append(copy)
+
+    for step in range(lines - 1):
+        came = line >= step + 1
+        index = jnp.maximum(line - 1 - step, 0) * 2 + side
+        swap = groups(index, {"gz": other})
+        pl.when(came)(lambda: wait_recv(rising[step][1]))
+        if step + 1 < lines - 1:
+            pl.when(rising[step + 1][0])(lambda: start(rising[step + 1][1]))
+        pl.when(came)(lambda: start(swap))
+        swaps.append((came, swap))
+        came = line + 1 + step < lines
+        index = jnp.minimum(line + 1 + step, lines - 1) * 2 + side
+        swap = groups(index, {"gz": other})
+        pl.when(came)(lambda: wait_recv(falling[step][1]))
+        if step + 1 < lines - 1:
+            pl.when(falling[step + 1][0])(lambda: start(falling[step + 1][1]))
+        pl.when(came)(lambda: start(swap))
+        swaps.append((came, swap))
+
+    pl.when(has_below)(down.wait_send)
+    pl.when(has_above)(up.wait_send)
+    for _, across, beside in sides:
+        across.wait_send()
+        beside.wait()
+    for copy in relays:
+        copy.wait()
+    for sent, copies in rising + falling:
+        pl.when(sent)(lambda: wait_send(copies))
+    for came, copies in swaps:
+        if came is None:
+            wait_send(copies)
+            wait_recv(copies)
+        else:
+            pl.when(came)(lambda: wait_send(copies))
+            pl.when(came)(lambda: wait_recv(copies))
+
+
+def spread(estimate, extra, dest, radius):
+    planes, rows_x, rows_y = estimate.shape
+    slabs = lax.axis_size("gz")
+    copies = 8 + 2 * (1 + 4 * (slabs // 2 - 1))
+    vmem = pl.BlockSpec(memory_space=pltpu.VMEM)
+    return pl.pallas_call(
+        spread_kernel,
+        out_shape=(
+            jax.ShapeDtypeStruct((planes + 2 * radius, rows_x, rows_y), jnp.bfloat16),
+            jax.ShapeDtypeStruct((slabs,) + extra.shape, extra.dtype),
+            jax.ShapeDtypeStruct((slabs,) + dest.shape, dest.dtype),
+        ),
+        in_specs=[vmem] * 3,
+        out_specs=(vmem,) * 3,
+        scratch_shapes=[
+            pltpu.SemaphoreType.DMA((copies,)),
+            pltpu.SemaphoreType.DMA((copies,)),
+        ],
+        compiler_params=pltpu.CompilerParams(
+            collective_id=2, has_side_effects=True, vmem_limit_bytes=VMEM_LIMIT
+        ),
+        cost_estimate=pl.CostEstimate(flops=0, bytes_accessed=120000000, transcendentals=0),
+        name="spread",
+    )(estimate, extra, dest)
+
+
 def place_kernel(source, main, extra, blocks):
     views, num = blocks.shape[:2]
     unroll = 8
@@ -113,20 +301,20 @@
     return target, placed, jnp.sum(same.astype(jnp.int32), axis=-1)
 
 
-def route(raw_views, block_dest):
-    view_num, blk_num = block_dest.shape
+def source_of(block_dest):
+    blk_num = block_dest.shape[1]
     slabs = lax.axis_size("gz")
     group = blk_num // slabs
-    me = lax.axis_index("gz")
-    dests = lax.all_gather(block_dest, "gz", axis=0)
-    dests, block_dest = lax.optimization_barrier((dests, block_dest))
-    target, placed, rank = slots_of(block_dest, blk_num, slabs)
+    target, _, rank = slots_of(block_dest, blk_num, slabs)
     slot = jnp.where(rank < group, target * group + rank, slabs * group + rank - group)
     hit = slot[:, None, :] == jnp.arange((slabs + 1) * group)[None, :, None]
-    source = jnp.sum(jnp.where(hit, jnp.arange(blk_num)[None, None, :], 0), axis=-1)
-    packed, extra = pack(source, raw_views, slabs, group)
-    main = lax.all_to_all(packed, "gz", split_axis=0, concat_axis=0, tiled=True)
-    late = lax.all_gather(extra, "gz", axis=0)
+    return jnp.sum(jnp.where(hit, jnp.arange(blk_num)[None, None, :], 0), axis=-1)
+
+
+def origin_of(dests):
+    slabs, view_num, blk_num = dests.shape
+    group = blk_num // slabs
+    me = lax.axis_index("gz")
     target, placed, rank = slots_of(dests, blk_num, slabs)
     slab_ids = jnp.arange(slabs)[:, None, None]
     code = slab_ids * 65536 + jnp.where(rank < group, rank, 256 + rank - group)
@@ -135,8 +323,7 @@
     where = jnp.where(target == me, placed, blk_num)
     where = jnp.swapaxes(where, 0, 1).reshape(view_num, slabs * blk_num)
     hit = where[:, None, :] == jnp.arange(blk_num)[None, :, None]
-    inverse = jnp.sum(jnp.where(hit, code[:, None, :], 0), axis=-1)
-    return place(inverse, main, late)
+    return jnp.sum(jnp.where(hit, code[:, None, :], 0), axis=-1)
 
 
 def exchange_kernel(last, partial, held, *refs):
@@ -356,11 +543,6 @@
     )(partial, held)
 
 
-def halo_of(quarter, radius):
-    planes = quarter.shape[0]
-    return shift(quarter[planes - radius:], "gz", 1), shift(quarter[:radius], "gz", -1)
-
-
 def body(estimate, raw_views, block_dest, lateral_psf, axial_psf):
     planes, rows_x, rows_y = estimate.shape
     along_x = normalize(lateral_psf[:, 0])
@@ -374,12 +556,11 @@
     rows_q = rows_x // parts
     mine = lax.axis_index("vert") * rows_q
     held = lax.dynamic_slice_in_dim(estimate, mine, rows_q, axis=1)
-    before, after = halo_of(held.astype(jnp.bfloat16), radius)
-    sides = lax.all_gather(jnp.concatenate([before, after], axis=0), "vert", axis=1, tiled=True)
-    widened = jnp.concatenate(
-        [sides[:radius], estimate.astype(jnp.bfloat16), sides[radius:]], axis=0
-    )
-    observed = route(raw_views, block_dest).reshape(-1, planes, rows_x, rows_y)
+    slabs = lax.axis_size("gz")
+    packed, extra = pack(source_of(block_dest), raw_views, slabs, block_dest.shape[1] // slabs)
+    main = lax.all_to_all(packed, "gz", split_axis=0, concat_axis=0, tiled=True)
+    widened, late, dests = spread(estimate, extra, block_dest, radius)
+    observed = place(origin_of(dests), main, late).reshape(-1, planes, rows_x, rows_y)
     for iteration in range(ITERS):
         first = jnp.einsum(
             "vzp,pxy->vzxy", front_matrix, widened, preferred_element_type=jnp.float32

time: 319 us -> 289 us (0.906)
  Pallas kernels: 98.3 us -> 209 us
  waiting for transfers between devices: 89.5 us -> 0.01 us
  blocking collectives: 27 us -> 0 us
  between operations: 13.6 us -> 0.19 us
  local copies, waits for them, and re-layouts: 26.9 us -> 22.2 us
    pallas_call x0 -> x1, Pallas kernels: none -> 113 us  [spread(): pl.pallas_call(spread_kernel, out_shape=(jax.ShapeDtypeStruct((planes + 2...]
    all_to_all x1, waiting for transfers between devices: 83.2 us -> 0.01 us  [body(): main = lax.all_to_all(packed, 'gz', split_axis=0, concat_axis=0, tiled=True)]
    all_gather x1 -> x0, blocking collectives: 27 us -> none  [route(): dests = lax.all_gather(block_dest, 'gz', axis=0)]
    ppermute x2 -> x0, starting transfers between devices: 6.14 us -> none  [shift(): return lax.ppermute(array, axis, pairs)]
    ppermute x2 -> x0, waiting for transfers between devices: 5.56 us -> none  [shift(): return lax.ppermute(array, axis, pairs)]
    all_to_all x1, starting transfers between devices: 3.65 us -> 7.38 us  [body(): main = lax.all_to_all(packed, 'gz', split_axis=0, concat_axis=0, tiled=True)]
    unnamed x18 -> x19, local copies, waits for them, and re-layouts: 7.45 us -> 3.8 us
  transfers between devices with their start and end apart: 5 -> 1, of which waited for: 3 -> 0; matrix products, arithmetic and copies ran while one was open for 7% -> 4% of each run, Pallas kernels for 1% -> 39%
where the time goes in v3:
time: 289 us; the launch traced here: 288 us
  Pallas kernels  209 us (72%)
  matrix products  34.9 us (12%)
  local copies, waits for them, and re-layouts  22.2 us (8%)
  other arithmetic  13.9 us (5%)
  starting transfers between devices  7.38 us (3%)
    pallas_call x1, Pallas kernels, spread(): pl.pallas_call(spread_kernel, out_shape=(jax.ShapeDtypeStruct((planes + 2...  113 us
    pallas_call x2, Pallas kernels, exchange(): pl.pallas_call(functools.partial(exchange_kernel, last), out_shape=out_sh...  85 us
    dot_general x2, matrix products, body(): jnp.einsum('vzxl,vjl->vzxj', second, mat_y, preferred_element_type=jnp.fl...  13.5 us
    dot_general x2, matrix products, body(): jnp.einsum('vik,vziy->vzky', mat_x, third, preferred_element_type=jnp.flo...  10.9 us
    convert_element_type x2, other arithmetic, body(): ratio = (observed.astype(jnp.float32) / blurred).astype(jnp.bfloat16)  10.4 us
    convert_element_type x2, local copies, waits for them, and re-layouts, body(): fourth = jnp.einsum('vik,vziy->vzky', mat_x, third, preferred_element_typ...  8.81 us
    dot_general x2, local copies, waits for them, and re-layouts, body(): jnp.einsum('vzp,vzxy->pxy', front_matrix, fourth, preferred_element_type=...  8.71 us
    pallas_call x1, Pallas kernels, place(): pl.pallas_call(place_kernel, out_shape=jax.ShapeDtypeStruct((views, slabs...  8.59 us
  transfers between devices with their start and end apart: 1, of which 0 were waited for; matrix products, arithmetic and copies ran while one was open for 4% of the time, Pallas kernels for 39%

profile of v3, /device:TPU:0, one launch (start us, length us, event | category | flops | bytes accessed | tf_op | source)
XLA Modules:
  0.0 287.9 jit_solution(5294683507448136962)
XLA Ops:
  0.0 0.7 add_select_fusion.2
  0.7 0.2 convert_reduce_fusion.1
  0.9 0.7 add_select_fusion.3
  1.8 2.9 %pack.1 = (bf16[8,3,16,16,256]{4,3,2,1,0:T(8,128)(2,1)S(1)}, bf16[3,16,16,256]{3,2,1,0:T(8,128)(2,1)S(1)}) custom-call(s32[3,144]{1,0:T(4,128)S(1)} %select_reduce_fusion.1.source, bf16[3,128,16,256]{3,2,1,0:T(8,128)(2,1)} %raw.1), custom_call_target="tpu_custom_call" | custom-call | tf_op jit(solution)/shard_map/pack/pallas_call | solution.py:53
  4.8 1.7 copy-done.1
  6.5 7.4 %all-to-all-start = ((bf16[8,3,16,16,256]{4,3,2,1,0:T(8,128)(2,1)}), bf16[8,3,16,16,256]{4,3,2,1,0:T(8,128)(2,1)}, u32[]{:S(2)}, u32[]{:S(2)}) async-start(bf16[8,3,16,16,256]{4,3,2,1,0:T(8,128)(2,1)} %copy-done.1), calls=%async_computation | async-start | bytes 6291456 | tf_op jit(solution)/shard_map/all_to_all | solution.py:561
  14.0 112.8 %spread.1 = (bf16[32,128,256]{2,1,0:T(8,128)(2,1)S(1)}, bf16[8,3,16,16,256]{4,3,2,1,0:T(8,128)(2,1)}, s32[8,3,128]{2,1,0:T(4,128)S(1)}) custom-call(f32[16,128,256]{2,1,0:T(8,128)S(1)} %copy-done, bf16[3,16,16,256]{3,2,1,0:T(8,128)(2,1)S(1)} %get-tuple-element.12.extra, s32[3,128]{1,0:T(4,128)S(1)} %copy-done.5), custom_call_target="tpu_custom_call" | custom-call | bytes 120000000 | tf_op jit(solution)/shard_map/spread/pallas_call | solution.py:242
  126.8 0.8 constant_dynamic-slice_fusion.held
  127.7 1.0 convert_reduce_fusion
  128.9 0.2 select_reduce_fusion.source
  129.2 0.2 fusion.41
  129.4 0.4 fusion.38
  129.8 2.1 fusion.2
  131.8 1.4 convolution_convert_fusion.1
  133.3 6.4 %fusion.5 = f32[3,16,128,256]{3,2,1,0:T(8,128)} fusion(bf16[3,16,128,256]{3,1,2,0:T(8,128)(2,1)S(1)} %convolution_convert_fusion.1, bf16[3,128,128]{2,0,1:T(4,128)(2,1)S(1)} %fusion.38, bf16[3,256,256]{2,0,1:T(4,128)(2,1)} %fusion.2), kind=kOutput, calls=%fused_computation.8 | convolution fusion | flops 1209532416 | bytes 9928704 | tf_op jit(solution)/shard_map/vzxl,vjl->vzxj/dot_general | solution.py:571
  139.6 8.6 %place.1 = bf16[3,128,16,256]{3,2,1,0:T(8,128)(2,1)S(1)} custom-call(s32[3,128]{1,0:T(4,128)S(1)} %select_reduce_fusion.source, bf16[8,3,16,16,256]{4,3,2,1,0:T(8,128)(2,1)} %all-to-all-done.main, bf16[8,3,16,16,256]{4,3,2,1,0:T(8,128)(2,1)} %get-tuple-element.15.extra), custom_call_target="tpu_custom_call" | custom-call | tf_op jit(solution)/shard_map/place/pallas_call | solution.py:285
  148.2 3.8 %fusion = bf16[3,16,128,256]{3,2,1,0:T(8,128)(2,1)} fusion(f32[3,16,128,256]{3,2,1,0:T(8,128)S(1)} %copy-done.6, bf16[3,16,128,256]{3,2,1,0:T(8,128)(2,1)S(1)} %bitcast.94), kind=kLoop, calls=%fused_computation.2 | loop fusion | flops 4718592 | bytes 12582912 | tf_op jit(solution)/shard_map/convert_element_type | solution.py:572
  152.1 5.4 %convert_bitcast_fusion.1 = bf16[3,16,128,256]{2,3,1,0:T(8,128)(2,1)} fusion(bf16[3,16,128,256]{3,2,1,0:T(8,128)(2,1)} %fusion, bf16[3,128,128]{2,0,1:T(4,128)(2,1)S(1)} %fusion.38, bf16[3,256,256]{2,0,1:T(4,128)(2,1)} %fusion.2), kind=kOutput, calls=%fused_computation.18 | convolution fusion | flops 1211105280 | bytes 6782976 | tf_op jit(solution)/shard_map/vik,vziy->vzky/dot_general | solution.py:576
  157.5 5.0 %copy.45 = bf16[3,16,128,256]{3,1,0,2:T(8,128)(2,1)} copy(bf16[3,16,128,256]{2,3,1,0:T(8,128)(2,1)} %convert_bitcast_fusion.1) | data formatting | bytes 6291456 | tf_op jit(solution)/shard_map/convert_element_type | solution.py:578
  162.5 2.6 convolution_bitcast_fusion.1
  165.1 4.4 %copy.46.partial = f32[32,128,256]{2,1,0:T(8,128)} copy(f32[32,128,256]{2,0,1:T(8,128)S(1)} %convolution_bitcast_fusion.1) | data formatting | bytes 8388608 | tf_op jit(solution)/shard_map/vzp,vzxy->pxy/dot_general | solution.py:579
  169.4 43.1 %renew.1 = (f32[16,32,256]{2,1,0:T(8,128)S(1)}, bf16[32,128,256]{2,1,0:T(8,128)(2,1)S(1)}) custom-call(f32[32,128,256]{2,1,0:T(8,128)} %copy.46.partial, f32[16,32,256]{2,1,0:T(8,128)S(1)} %copy-done.2), custom_call_target="tpu_custom_call" | custom-call | tf_op jit(solution)/shard_map/renew/pallas_call | solution.py:525
  212.6 0.8 copy-done.3
  213.4 3.1 %convolution_convert_fusion = bf16[3,16,128,256]{3,1,2,0:T(8,128)(2,1)} fusion(bf16[32,128,256]{2,1,0:T(8,128)(2,1)S(1)} %get-tuple-element.17, bf16[3,16,32]{2,0,1:T(4,128)(2,1)S(1)} %fusion.41), kind=kOutput, calls=%fused_computation.25 | convolution fusion | flops 102236160 | bytes 5245952 | tf_op jit(solution)/shard_map/vzp,pxy->vzxy/dot_general | solution.py:565
  216.5 7.2 %fusion.3 = f32[3,16,128,256]{3,2,1,0:T(8,128)} fusion(bf16[3,16,128,256]{3,1,2,0:T(8,128)(2,1)} %convolution_convert_fusion, bf16[3,128,128]{2,0,1:T(4,128)(2,1)S(1)} %fusion.38, bf16[3,256,256]{2,0,1:T(4,128)(2,1)} %fusion.2), kind=kOutput, calls=%fused_computation.6 | convolution fusion | flops 1209532416 | bytes 9928704 | tf_op jit(solution)/shard_map/vzxl,vjl->vzxj/dot_general | solution.py:571
  223.7 6.6 %fusion.1 = bf16[3,16,128,256]{3,2,1,0:T(8,128)(2,1)} fusion(f32[3,16,128,256]{3,2,1,0:T(8,128)} %fusion.3, bf16[3,16,128,256]{3,2,1,0:T(8,128)(2,1)S(1)} %bitcast.95), kind=kLoop, calls=%fused_computation.3 | loop fusion | flops 4718592 | bytes 12582912 | tf_op jit(solution)/shard_map/convert_element_type | solution.py:572
  230.3 5.5 %convert_bitcast_fusion = bf16[3,16,128,256]{2,3,1,0:T(8,128)(2,1)} fusion(bf16[3,16,128,256]{3,2,1,0:T(8,128)(2,1)} %fusion.1, bf16[3,128,128]{2,0,1:T(4,128)(2,1)S(1)} %fusion.38, bf16[3,256,256]{2,0,1:T(4,128)(2,1)} %fusion.2), kind=kOutput, calls=%fused_computation.14 | convolution fusion | flops 1211105280 | bytes 6782976 | tf_op jit(solution)/shard_map/vik,vziy->vzky/dot_general | solution.py:576
  235.7 3.9 %copy.51 = bf16[3,16,128,256]{3,1,0,2:T(8,128)(2,1)S(1)} copy(bf16[3,16,128,256]{2,3,1,0:T(8,128)(2,1)} %convert_bitcast_fusion) | data formatting | bytes 6291456 | tf_op jit(solution)/shard_map/convert_element_type | solution.py:578
  239.6 0.7 convolution_bitcast_fusion
  240.3 4.4 %copy.52.partial = f32[32,128,256]{2,1,0:T(8,128)} copy(f32[32,128,256]{2,0,1:T(8,128)S(1)} %convolution_bitcast_fusion) | data formatting | bytes 8388608 | tf_op jit(solution)/shard_map/vzp,vzxy->pxy/dot_general | solution.py:579
  244.7 41.9 %finish.1 = f32[16,128,256]{2,1,0:T(8,128)S(1)} custom-call(f32[32,128,256]{2,1,0:T(8,128)} %copy.52.partial, f32[16,32,256]{2,1,0:T(8,128)S(1)} %copy-done.4), custom_call_target="tpu_custom_call" | custom-call | tf_op jit(solution)/shard_map/finish/pallas_call | solution.py:525
  286.6 1.3 copy.133
  (27 shorter events, 0.6 us)
Async XLA Ops:
  4.8 1.7 copy-start.1
  6.4 7.4 %copy-start.8 = (f32[3,17]{1,0:T(4,128)S(1)}, f32[3,17]{1,0:T(4,128)}, u32[]{:S(2)}) copy-start(f32[3,17]{1,0:T(4,128)} %param.9) | copy-start | bytes 616
  6.5 7.5 %copy-start = (f32[16,128,256]{2,1,0:T(8,128)S(1)}, f32[16,128,256]{2,1,0:T(8,128)}, u32[]{:S(2)}) copy-start(f32[16,128,256]{2,1,0:T(8,128)} %estimate.1) | copy-start | bytes 6291460
  6.5 7.5 %copy-start.5 = (s32[3,128]{1,0:T(4,128)S(1)}, s32[3,128]{1,0:T(4,128)}, u32[]{:S(2)}) copy-start(s32[3,128]{1,0:T(4,128)} %dest.1) | copy-start | bytes 4612
  6.5 133.2 %all-to-all-start = ((bf16[8,3,16,16,256]{4,3,2,1,0:T(8,128)(2,1)}), bf16[8,3,16,16,256]{4,3,2,1,0:T(8,128)(2,1)}, u32[]{:S(2)}, u32[]{:S(2)}) async-start(bf16[8,3,16,16,256]{4,3,2,1,0:T(8,128)(2,1)} %copy-done.1), calls=%async_computation | async-start | bytes 6291456 | tf_op jit(solution)/shard_map/all_to_all | solution.py:561
  13.8 115.3 %copy-start.7 = (f32[3,2,17]{2,1,0:T(2,128)S(1)}, f32[3,2,17]{2,1,0:T(2,128)}, u32[]{:S(2)}) copy-start(f32[3,2,17]{2,1,0:T(2,128)} %param.8) | copy-start | bytes 1228
  139.6 8.6 %copy-start.6 = (f32[3,16,128,256]{3,2,1,0:T(8,128)S(1)}, f32[3,16,128,256]{3,2,1,0:T(8,128)}, u32[]{:S(2)}) copy-start(f32[3,16,128,256]{3,2,1,0:T(8,128)} %fusion.5) | copy-start | bytes 18874372
  165.1 4.4 %copy-start.2 = (f32[16,32,256]{2,1,0:T(8,128)S(1)}, f32[16,32,256]{2,1,0:T(8,128)}, u32[]{:S(2)}) copy-start(f32[16,32,256]{2,1,0:T(8,128)} %constant_dynamic-slice_fusion.held) | copy-start | bytes 1572868
  212.6 0.8 copy-start.3
  240.3 4.4 %copy-start.4 = (f32[16,32,256]{2,1,0:T(8,128)S(1)}, f32[16,32,256]{2,1,0:T(8,128)}, u32[]{:S(2)}) copy-start(f32[16,32,256]{2,1,0:T(8,128)} %copy-done.3) | copy-start | bytes 1572868

commit v4 on v3

--- a/solution.py
+++ b/solution.py
@@ -63,7 +63,9 @@
     )(source, raw)
 
 
-def spread_kernel(estimate, extra, dest, widened, late, dests, send_sem, recv_sem):
+def spread_kernel(
+    estimate, packed, extra, dest, widened, main, late, dests, send_sem, recv_sem
+):
     planes, rows_x, rows_y = estimate.shape
     radius = (widened.shape[0] - planes) // 2
     slab, slabs = lax.axis_index("gz"), lax.axis_size("gz")
@@ -118,18 +120,18 @@
 
     greet({"vert": near})
     greet({"vert": far})
-    pl.when(has_below)(lambda: greet({"gz": slab - 1}))
-    pl.when(has_above)(lambda: greet({"gz": slab + 1}))
-    pl.when(line_below)(lambda: greet({"gz": slab - 2}))
-    pl.when(line_above)(lambda: greet({"gz": slab + 2}))
-    pl.semaphore_wait(
-        barrier,
-        2
-        + jnp.minimum(slab, 1)
-        + jnp.minimum(slabs - 1 - slab, 1)
-        + jnp.minimum(line, 1)
-        + jnp.minimum(lines - 1 - line, 1),
-    )
+
+    def peer(distance):
+        found, bit = slab, 1
+        while bit < slabs:
+            if distance & bit:
+                found = found + bit - 2 * bit * ((slab // bit) % 2)
+            bit *= 2
+        return found
+
+    for distance in range(1, slabs):
+        greet({"gz": peer(distance)})
+    pl.semaphore_wait(barrier, slabs + 1)
 
     for edge in (0, planes - radius):
         widened[pl.ds(radius + edge, radius), rows(part)] = estimate[
@@ -156,6 +158,13 @@
     pl.when(rising[0][0])(lambda: start(rising[0][1]))
     pl.when(falling[0][0])(lambda: start(falling[0][1]))
     start(swaps[0][1])
+
+    groups_sent = []
+    for distance in range(slabs - 1, 0, -1):
+        copy = remote(packed.at[peer(distance)], main.at[slab], {"gz": peer(distance)})
+        copy.start()
+        groups_sent.append(copy)
+    main[slab] = packed[slab]
 
     @pl.when(jnp.logical_not(has_below))
     def _():
@@ -232,22 +241,26 @@
         else:
             pl.when(came)(lambda: wait_send(copies))
             pl.when(came)(lambda: wait_recv(copies))
-
-
-def spread(estimate, extra, dest, radius):
+    for copy in groups_sent:
+        copy.wait_send()
+        copy.wait_recv()
+
+
+def spread(estimate, packed, extra, dest, radius):
     planes, rows_x, rows_y = estimate.shape
     slabs = lax.axis_size("gz")
-    copies = 8 + 2 * (1 + 4 * (slabs // 2 - 1))
+    copies = 8 + 2 * (1 + 4 * (slabs // 2 - 1)) + slabs - 1
     vmem = pl.BlockSpec(memory_space=pltpu.VMEM)
     return pl.pallas_call(
         spread_kernel,
         out_shape=(
             jax.ShapeDtypeStruct((planes + 2 * radius, rows_x, rows_y), jnp.bfloat16),
+            jax.ShapeDtypeStruct(packed.shape, packed.dtype),
             jax.ShapeDtypeStruct((slabs,) + extra.shape, extra.dtype),
             jax.ShapeDtypeStruct((slabs,) + dest.shape, dest.dtype),
         ),
-        in_specs=[vmem] * 3,
-        out_specs=(vmem,) * 3,
+        in_specs=[vmem] * 4,
+        out_specs=(vmem,) * 4,
         scratch_shapes=[
             pltpu.SemaphoreType.DMA((copies,)),
             pltpu.SemaphoreType.DMA((copies,)),
@@ -255,9 +268,8 @@
         compiler_params=pltpu.CompilerParams(
             collective_id=2, has_side_effects=True, vmem_limit_bytes=VMEM_LIMIT
         ),
-        cost_estimate=pl.CostEstimate(flops=0, bytes_accessed=120000000, transcendentals=0),
         name="spread",
-    )(estimate, extra, dest)
+    )(estimate, packed, extra, dest)
 
 
 def place_kernel(source, main, extra, blocks):
@@ -332,7 +344,7 @@
     else:
         (renewed, result, got_a, forward, got_b, edge, got_halo, send_sem, recv_sem) = refs
     planes, rows_q, _ = held.shape
-    radius = edge.shape[1]
+    radius = edge.shape[2]
     half = planes // 2
     slab, slabs = lax.axis_index("gz"), lax.axis_size("gz")
     part, parts = lax.axis_index("vert"), lax.axis_size("vert")
@@ -377,9 +389,9 @@
     waits = []
     stage_a = []
     for chunk in chunks:
-        passing = remote(partial.at[chunk, rows(near_far)], got_a.at[1, chunk], {"vert": near})
+        passing = remote(partial.at[rows(near_far), chunk], got_a.at[1, :, chunk], {"vert": near})
         passing.start()
-        staying = remote(partial.at[chunk, rows(near)], got_a.at[0, chunk], {"vert": near})
+        staying = remote(partial.at[rows(near), chunk], got_a.at[0, :, chunk], {"vert": near})
         staying.start()
         stage_a.append((passing, staying))
         waits += [passing, staying]
@@ -409,8 +421,8 @@
     stage_b = []
     for chunk, (passing, _) in zip(chunks, stage_a):
         passing.wait_recv()
-        forward[chunk] = partial[chunk, rows(far)] + got_a[1, chunk]
-        copy = remote(forward.at[chunk], got_b.at[chunk], {"vert": far})
+        forward[:, chunk] = partial[rows(far), chunk] + got_a[1, :, chunk]
+        copy = remote(forward.at[:, chunk], got_b.at[:, chunk], {"vert": far})
         copy.start()
         stage_b.append(copy)
         waits.append(copy)
@@ -419,7 +431,7 @@
         chunk = chunks[place]
         stage_a[place][1].wait_recv()
         stage_b[place].wait_recv()
-        return (partial[chunk, rows(part)] + got_a[0, chunk]) + got_b[chunk]
+        return (partial[rows(part), chunk] + got_a[0, :, chunk]) + got_b[:, chunk]
 
     edge[0] = total(0)
     down = remote(edge.at[0], got_halo.at[1], {"gz": slab - 1})
@@ -439,7 +451,7 @@
         else:
             pl.when(has_above)(lambda: down.wait_recv())
         own = pl.ds(place * half, half)
-        value = held[own] * (summed + got_halo[place]) / VIEWS
+        value = held[own] * jnp.swapaxes(summed + got_halo[place], 0, 1) / VIEWS
         if not last:
             renewed[own] = value
         target = result.at[pl.ds(inner + place * half, half), rows(part)]
@@ -506,7 +518,7 @@
 
 
 def exchange(partial, held, last):
-    whole, rows_x, rows_y = partial.shape
+    rows_x, whole, rows_y = partial.shape
     planes, rows_q, _ = held.shape
     radius = (whole - planes) // 2
     assert planes == 2 * radius and rows_x == 4 * rows_q
@@ -528,11 +540,11 @@
         in_specs=[vmem, vmem],
         out_specs=out_specs,
         scratch_shapes=[
-            pltpu.VMEM((2, whole, rows_q, rows_y), f32),
-            pltpu.VMEM((whole, rows_q, rows_y), f32),
-            pltpu.VMEM((whole, rows_q, rows_y), f32),
-            pltpu.VMEM((2, radius, rows_q, rows_y), f32),
-            pltpu.VMEM((2, radius, rows_q, rows_y), f32),
+            pltpu.VMEM((2, rows_q, whole, rows_y), f32),
+            pltpu.VMEM((rows_q, whole, rows_y), f32),
+            pltpu.VMEM((rows_q, whole, rows_y), f32),
+            pltpu.VMEM((2, rows_q, radius, rows_y), f32),
+            pltpu.VMEM((2, rows_q, radius, rows_y), f32),
             pltpu.SemaphoreType.DMA((copies,)),
             pltpu.SemaphoreType.DMA((copies,)),
         ],
@@ -558,8 +570,7 @@
     held = lax.dynamic_slice_in_dim(estimate, mine, rows_q, axis=1)
     slabs = lax.axis_size("gz")
     packed, extra = pack(source_of(block_dest), raw_views, slabs, block_dest.shape[1] // slabs)
-    main = lax.all_to_all(packed, "gz", split_axis=0, concat_axis=0, tiled=True)
-    widened, late, dests = spread(estimate, extra, block_dest, radius)
+    widened, main, late, dests = spread(estimate, packed, extra, block_dest, radius)
     observed = place(origin_of(dests), main, late).reshape(-1, planes, rows_x, rows_y)
     for iteration in range(ITERS):
         first = jnp.einsum(
@@ -577,7 +588,7 @@
             "vik,vziy->vzky", mat_x, third, preferred_element_type=jnp.float32
         ).astype(jnp.bfloat16)
         partial_back = jnp.einsum(
-            "vzp,vzxy->pxy", front_matrix, fourth, preferred_element_type=jnp.float32
+            "vzp,vzxy->xpy", front_matrix, fourth, preferred_element_type=jnp.float32
         )
         if iteration < ITERS - 1:
             held, widened = exchange(partial_back, held, False)

time: 289 us -> 294 us (1.017)
  Pallas kernels: 209 us -> 219 us
  local copies, waits for them, and re-layouts: 22.2 us -> 14.4 us
  starting transfers between devices: 7.38 us -> 0 us
  matrix products: 34.9 us -> 42.1 us
  other arithmetic: 13.9 us -> 17.9 us
    dot_general x2 -> x0, local copies, waits for them, and re-layouts: 8.71 us -> none  [body(): jnp.einsum('vzp,vzxy->pxy', front_matrix, fourth, preferred_element_type=...]
    pallas_call x1, Pallas kernels: 113 us -> 121 us  [spread(): pl.pallas_call(spread_kernel, out_shape=(jax.ShapeDtypeStruct((planes + 2...]
    all_to_all x1 -> x0, starting transfers between devices: 7.38 us -> none  [body(): main = lax.all_to_all(packed, 'gz', split_axis=0, concat_axis=0, tiled=True)]
    dot_general x2, matrix products: 3.35 us -> 7.3 us  [body(): jnp.einsum('vzp,vzxy->xpy', front_matrix, fourth, preferred_element_type=...]
  transfers between devices with their start and end apart: 1 -> 0, of which waited for: 0 -> 0; matrix products, arithmetic and copies ran while one was open for 4% -> 0% of each run, Pallas kernels for 39% -> 0%
where the time goes in v4:
time: 294 us
  Pallas kernels  219 us (74%)
  matrix products  42.1 us (14%)
  other arithmetic  17.9 us (6%)
  local copies, waits for them, and re-layouts  14.4 us (5%)
    pallas_call x1, Pallas kernels, spread(): pl.pallas_call(spread_kernel, out_shape=(jax.ShapeDtypeStruct((planes + 2...  121 us
    pallas_call x2, Pallas kernels, exchange(): pl.pallas_call(functools.partial(exchange_kernel, last), out_shape=out_sh...  87 us
    dot_general x2, matrix products, body(): jnp.einsum('vzxl,vjl->vzxj', second, mat_y, preferred_element_type=jnp.fl...  14.4 us
    convert_element_type x2, other arithmetic, body(): ratio = (observed.astype(jnp.float32) / blurred).astype(jnp.bfloat16)  13 us
    dot_general x2, matrix products, body(): jnp.einsum('vik,vziy->vzky', mat_x, third, preferred_element_type=jnp.flo...  10.9 us
    convert_element_type x2, local copies, waits for them, and re-layouts, body(): fourth = jnp.einsum('vik,vziy->vzky', mat_x, third, preferred_element_typ...  8.78 us
    pallas_call x1, Pallas kernels, place(): pl.pallas_call(place_kernel, out_shape=jax.ShapeDtypeStruct((views, slabs...  8.45 us
    dot_general x2, matrix products, body(): jnp.einsum('vzp,vzxy->xpy', front_matrix, fourth, preferred_element_type=...  7.3 us

profile of v4, /device:TPU:0, one launch (start us, length us, event | category | flops | bytes accessed | tf_op | source)
XLA Modules:
  0.0 293.8 jit_solution(8476036477978327269)
XLA Ops:
  0.0 0.8 reduce_sum.67
  0.8 0.7 add_select_fusion.2
  1.5 0.9 slice_reduce_fusion
  2.4 0.9 fusion.41
  3.3 0.2 convert_reduce_fusion.1
  3.5 0.7 add_select_fusion.3
  4.2 0.2 select_reduce_fusion.1.source
  4.4 0.4 fusion.38
  4.9 2.1 fusion.2
  6.9 1.9 constant_dynamic-slice_fusion.held
  8.8 2.9 %pack.1 = (bf16[8,3,16,16,256]{4,3,2,1,0:T(8,128)(2,1)S(1)}, bf16[3,16,16,256]{3,2,1,0:T(8,128)(2,1)S(1)}) custom-call(s32[3,144]{1,0:T(4,128)S(1)} %select_reduce_fusion.1.source, bf16[3,128,16,256]{3,2,1,0:T(8,128)(2,1)} %raw.1), custom_call_target="tpu_custom_call" | custom-call | tf_op jit(solution)/shard_map/pack/pallas_call | solution.py:53
  11.7 1.7 copy-done.1
  13.4 120.8 %spread.1 = (bf16[32,128,256]{2,1,0:T(8,128)(2,1)S(1)}, bf16[8,3,16,16,256]{4,3,2,1,0:T(8,128)(2,1)}, bf16[8,3,16,16,256]{4,3,2,1,0:T(8,128)(2,1)}, s32[8,3,128]{2,1,0:T(4,128)S(1)}) custom-call(f32[16,128,256]{2,1,0:T(8,128)S(1)} %copy-done, bf16[8,3,16,16,256]{4,3,2,1,0:T(8,128)(2,1)} %copy-done.1, bf16[3,16,16,256]{3,2,1,0:T(8,128)(2,1)S(1)} %get-tuple-element.14.extra, ...), custom_call_target="tpu_custom_call" | custom-call | tf_op jit(solution)/shard_map/spread/pallas_call | solution.py:254
  134.2 1.0 convert_reduce_fusion
  135.4 0.2 select_reduce_fusion.source
  135.6 8.4 %place.1 = bf16[3,128,16,256]{3,2,1,0:T(8,128)(2,1)S(1)} custom-call(s32[3,128]{1,0:T(4,128)S(1)} %select_reduce_fusion.source, bf16[8,3,16,16,256]{4,3,2,1,0:T(8,128)(2,1)} %get-tuple-element.16.main, bf16[8,3,16,16,256]{4,3,2,1,0:T(8,128)(2,1)} %get-tuple-element.17.extra), custom_call_target="tpu_custom_call" | custom-call | tf_op jit(solution)/shard_map/place/pallas_call | solution.py:297
  144.1 3.1 %convolution_convert_fusion.1 = bf16[3,16,128,256]{3,1,2,0:T(8,128)(2,1)} fusion(bf16[32,128,256]{2,1,0:T(8,128)(2,1)S(1)} %get-tuple-element.18, bf16[3,16,32]{2,0,1:T(4,128)(2,1)S(1)} %fusion.41), kind=kOutput, calls=%fused_computation.26 | convolution fusion | flops 102236160 | bytes 5245952 | tf_op jit(solution)/shard_map/vzp,pxy->vzxy/dot_general | solution.py:576
  147.2 7.2 %fusion.5 = f32[3,16,128,256]{3,2,1,0:T(8,128)} fusion(bf16[3,16,128,256]{3,1,2,0:T(8,128)(2,1)} %convolution_convert_fusion.1, bf16[3,128,128]{2,0,1:T(4,128)(2,1)S(1)} %fusion.38, bf16[3,256,256]{2,0,1:T(4,128)(2,1)} %fusion.2), kind=kOutput, calls=%fused_computation.8 | convolution fusion | flops 1209532416 | bytes 9928704 | tf_op jit(solution)/shard_map/vzxl,vjl->vzxj/dot_general | solution.py:582
  154.4 6.5 %fusion = bf16[3,16,128,256]{3,2,1,0:T(8,128)(2,1)} fusion(f32[3,16,128,256]{3,2,1,0:T(8,128)} %fusion.5, bf16[3,16,128,256]{3,2,1,0:T(8,128)(2,1)S(1)} %bitcast.98), kind=kLoop, calls=%fused_computation.2 | loop fusion | flops 4718592 | bytes 12582912 | tf_op jit(solution)/shard_map/convert_element_type | solution.py:583
  160.9 5.5 %convert_bitcast_fusion.1 = bf16[3,16,128,256]{2,3,1,0:T(8,128)(2,1)} fusion(bf16[3,16,128,256]{3,2,1,0:T(8,128)(2,1)} %fusion, bf16[3,128,128]{2,0,1:T(4,128)(2,1)S(1)} %fusion.38, bf16[3,256,256]{2,0,1:T(4,128)(2,1)} %fusion.2), kind=kOutput, calls=%fused_computation.18 | convolution fusion | flops 1211105280 | bytes 6782976 | tf_op jit(solution)/shard_map/vik,vziy->vzky/dot_general | solution.py:587
  166.3 4.9 %copy.39 = bf16[3,16,128,256]{3,1,0,2:T(8,128)(2,1)} copy(bf16[3,16,128,256]{2,3,1,0:T(8,128)(2,1)} %convert_bitcast_fusion.1) | data formatting | bytes 6291456 | tf_op jit(solution)/shard_map/convert_element_type | solution.py:589
  171.3 4.6 %convolution_bitcast_fusion.1.partial = f32[128,32,256]{2,1,0:T(8,128)} fusion(bf16[3,16,128,256]{3,1,0,2:T(8,128)(2,1)} %copy.39, bf16[3,16,32]{2,0,1:T(4,128)(2,1)S(1)} %fusion.41), kind=kOutput, calls=%fused_computation.28 | convolution fusion | flops 100663296 | bytes 7343104 | tf_op jit(solution)/shard_map/vzp,vzxy->xpy/dot_general | solution.py:590
  175.9 44.4 %renew.1 = (f32[16,32,256]{2,1,0:T(8,128)S(1)}, bf16[32,128,256]{2,1,0:T(8,128)(2,1)S(1)}) custom-call(f32[128,32,256]{2,1,0:T(8,128)} %convolution_bitcast_fusion.1.partial, f32[16,32,256]{2,1,0:T(8,128)S(1)} %copy-done.2), custom_call_target="tpu_custom_call" | custom-call | tf_op jit(solution)/shard_map/renew/pallas_call | solution.py:537
  220.3 0.8 copy-done.3
  221.1 3.1 %convolution_convert_fusion = bf16[3,16,128,256]{3,1,2,0:T(8,128)(2,1)} fusion(bf16[32,128,256]{2,1,0:T(8,128)(2,1)S(1)} %get-tuple-element.19, bf16[3,16,32]{2,0,1:T(4,128)(2,1)S(1)} %fusion.41), kind=kOutput, calls=%fused_computation.25 | convolution fusion | flops 102236160 | bytes 5245952 | tf_op jit(solution)/shard_map/vzp,pxy->vzxy/dot_general | solution.py:576
  224.2 7.2 %fusion.3 = f32[3,16,128,256]{3,2,1,0:T(8,128)} fusion(bf16[3,16,128,256]{3,1,2,0:T(8,128)(2,1)} %convolution_convert_fusion, bf16[3,128,128]{2,0,1:T(4,128)(2,1)S(1)} %fusion.38, bf16[3,256,256]{2,0,1:T(4,128)(2,1)} %fusion.2), kind=kOutput, calls=%fused_computation.6 | convolution fusion | flops 1209532416 | bytes 9928704 | tf_op jit(solution)/shard_map/vzxl,vjl->vzxj/dot_general | solution.py:582
  231.4 6.5 %fusion.1 = bf16[3,16,128,256]{3,2,1,0:T(8,128)(2,1)} fusion(f32[3,16,128,256]{3,2,1,0:T(8,128)} %fusion.3, bf16[3,16,128,256]{3,2,1,0:T(8,128)(2,1)S(1)} %bitcast.99), kind=kLoop, calls=%fused_computation.3 | loop fusion | flops 4718592 | bytes 12582912 | tf_op jit(solution)/shard_map/convert_element_type | solution.py:583
  237.9 5.5 %convert_bitcast_fusion = bf16[3,16,128,256]{2,3,1,0:T(8,128)(2,1)} fusion(bf16[3,16,128,256]{3,2,1,0:T(8,128)(2,1)} %fusion.1, bf16[3,128,128]{2,0,1:T(4,128)(2,1)S(1)} %fusion.38, bf16[3,256,256]{2,0,1:T(4,128)(2,1)} %fusion.2), kind=kOutput, calls=%fused_computation.14 | convolution fusion | flops 1211105280 | bytes 6782976 | tf_op jit(solution)/shard_map/vik,vziy->vzky/dot_general | solution.py:587
  243.4 3.9 %copy.44 = bf16[3,16,128,256]{3,1,0,2:T(8,128)(2,1)S(1)} copy(bf16[3,16,128,256]{2,3,1,0:T(8,128)(2,1)} %convert_bitcast_fusion) | data formatting | bytes 6291456 | tf_op jit(solution)/shard_map/convert_element_type | solution.py:589
  247.3 2.7 convolution_bitcast_fusion.partial
  249.9 42.6 %finish.1 = f32[16,128,256]{2,1,0:T(8,128)S(1)} custom-call(f32[128,32,256]{2,1,0:T(8,128)} %convolution_bitcast_fusion.partial, f32[16,32,256]{2,1,0:T(8,128)S(1)} %copy-done.4), custom_call_target="tpu_custom_call" | custom-call | tf_op jit(solution)/shard_map/finish/pallas_call | solution.py:537
  292.5 1.3 copy.125
  (17 shorter events, 0.2 us)
Async XLA Ops:
  4.8 8.6 %copy-start = (f32[16,128,256]{2,1,0:T(8,128)S(1)}, f32[16,128,256]{2,1,0:T(8,128)}, u32[]{:S(2)}) copy-start(f32[16,128,256]{2,1,0:T(8,128)} %estimate.1) | copy-start | bytes 6291460
  4.8 8.6 %copy-start.5 = (s32[3,128]{1,0:T(4,128)S(1)}, s32[3,128]{1,0:T(4,128)}, u32[]{:S(2)}) copy-start(s32[3,128]{1,0:T(4,128)} %dest.1) | copy-start | bytes 4612
  11.7 1.7 copy-start.1
  171.3 4.6 %copy-start.2 = (f32[16,32,256]{2,1,0:T(8,128)S(1)}, f32[16,32,256]{2,1,0:T(8,128)}, u32[]{:S(2)}) copy-start(f32[16,32,256]{2,1,0:T(8,128)} %constant_dynamic-slice_fusion.held) | copy-start | bytes 1572868
  220.3 0.8 copy-start.3
  247.2 2.7 copy-start.4

commit v5 on v4

--- a/solution.py
+++ b/solution.py
@@ -161,9 +161,10 @@
 
     groups_sent = []
     for distance in range(slabs - 1, 0, -1):
-        copy = remote(packed.at[peer(distance)], main.at[slab], {"gz": peer(distance)})
-        copy.start()
-        groups_sent.append(copy)
+        groups_sent.append(
+            remote(packed.at[peer(distance)], main.at[slab], {"gz": peer(distance)})
+        )
+    groups_sent[0].start()
     main[slab] = packed[slab]
 
     @pl.when(jnp.logical_not(has_below))
@@ -224,6 +225,10 @@
             pl.when(falling[step + 1][0])(lambda: start(falling[step + 1][1]))
         pl.when(came)(lambda: start(swap))
         swaps.append((came, swap))
+        if step + 1 < lines - 1:
+            groups_sent[step + 1].start()
+        else:
+            start(groups_sent[step + 1:])
 
     pl.when(has_below)(down.wait_send)
     pl.when(has_above)(up.wait_send)

time: 294 us -> 280 us (0.952)
  Pallas kernels: 219 us -> 205 us
    pallas_call x1, Pallas kernels: 121 us -> 108 us  [spread(): pl.pallas_call(spread_kernel, out_shape=(jax.ShapeDtypeStruct((planes + 2...]
where the time goes in v5:
time: 280 us
  Pallas kernels  205 us (73%)
  matrix products  42.1 us (15%)
  other arithmetic  17.9 us (6%)
  local copies, waits for them, and re-layouts  14.4 us (5%)
    pallas_call x1, Pallas kernels, spread(): pl.pallas_call(spread_kernel, out_shape=(jax.ShapeDtypeStruct((planes + 2...  108 us
    pallas_call x2, Pallas kernels, exchange(): pl.pallas_call(functools.partial(exchange_kernel, last), out_shape=out_sh...  85.4 us
    dot_general x2, matrix products, body(): jnp.einsum('vzxl,vjl->vzxj', second, mat_y, preferred_element_type=jnp.fl...  14.4 us
    convert_element_type x2, other arithmetic, body(): ratio = (observed.astype(jnp.float32) / blurred).astype(jnp.bfloat16)  13 us
    dot_general x2, matrix products, body(): jnp.einsum('vik,vziy->vzky', mat_x, third, preferred_element_type=jnp.flo...  10.9 us
    convert_element_type x2, local copies, waits for them, and re-layouts, body(): fourth = jnp.einsum('vik,vziy->vzky', mat_x, third, preferred_element_typ...  8.78 us
    pallas_call x1, Pallas kernels, place(): pl.pallas_call(place_kernel, out_shape=jax.ShapeDtypeStruct((views, slabs...  8.45 us
    dot_general x2, matrix products, body(): jnp.einsum('vzp,vzxy->xpy', front_matrix, fourth, preferred_element_type=...  7.3 us

profile of v5, /device:TPU:0, one launch (start us, length us, event | category | flops | bytes accessed | tf_op | source)
XLA Modules:
  0.0 279.7 jit_solution(10785124291929454317)
XLA Ops:
  0.0 0.8 reduce_sum.67
  0.8 0.7 add_select_fusion.2
  1.5 0.9 slice_reduce_fusion
  2.4 0.9 fusion.41
  3.3 0.2 convert_reduce_fusion.1
  3.5 0.7 add_select_fusion.3
  4.2 0.2 select_reduce_fusion.1.source
  4.4 0.4 fusion.38
  4.9 2.1 fusion.2
  6.9 1.9 constant_dynamic-slice_fusion.held
  8.8 2.9 %pack.1 = (bf16[8,3,16,16,256]{4,3,2,1,0:T(8,128)(2,1)S(1)}, bf16[3,16,16,256]{3,2,1,0:T(8,128)(2,1)S(1)}) custom-call(s32[3,144]{1,0:T(4,128)S(1)} %select_reduce_fusion.1.source, bf16[3,128,16,256]{3,2,1,0:T(8,128)(2,1)} %raw.1), custom_call_target="tpu_custom_call" | custom-call | tf_op jit(solution)/shard_map/pack/pallas_call | solution.py:53
  11.7 1.7 copy-done.1
  13.4 108.3 %spread.1 = (bf16[32,128,256]{2,1,0:T(8,128)(2,1)S(1)}, bf16[8,3,16,16,256]{4,3,2,1,0:T(8,128)(2,1)}, bf16[8,3,16,16,256]{4,3,2,1,0:T(8,128)(2,1)}, s32[8,3,128]{2,1,0:T(4,128)S(1)}) custom-call(f32[16,128,256]{2,1,0:T(8,128)S(1)} %copy-done, bf16[8,3,16,16,256]{4,3,2,1,0:T(8,128)(2,1)} %copy-done.1, bf16[3,16,16,256]{3,2,1,0:T(8,128)(2,1)S(1)} %get-tuple-element.14.extra, ...), custom_call_target="tpu_custom_call" | custom-call | tf_op jit(solution)/shard_map/spread/pallas_call | solution.py:259
  121.8 1.0 convert_reduce_fusion
  122.9 0.2 select_reduce_fusion.source
  123.1 8.4 %place.1 = bf16[3,128,16,256]{3,2,1,0:T(8,128)(2,1)S(1)} custom-call(s32[3,128]{1,0:T(4,128)S(1)} %select_reduce_fusion.source, bf16[8,3,16,16,256]{4,3,2,1,0:T(8,128)(2,1)} %get-tuple-element.16.main, bf16[8,3,16,16,256]{4,3,2,1,0:T(8,128)(2,1)} %get-tuple-element.17.extra), custom_call_target="tpu_custom_call" | custom-call | tf_op jit(solution)/shard_map/place/pallas_call | solution.py:302
  131.6 3.1 %convolution_convert_fusion.1 = bf16[3,16,128,256]{3,1,2,0:T(8,128)(2,1)} fusion(bf16[32,128,256]{2,1,0:T(8,128)(2,1)S(1)} %get-tuple-element.18, bf16[3,16,32]{2,0,1:T(4,128)(2,1)S(1)} %fusion.41), kind=kOutput, calls=%fused_computation.26 | convolution fusion | flops 102236160 | bytes 5245952 | tf_op jit(solution)/shard_map/vzp,pxy->vzxy/dot_general | solution.py:581
  134.7 7.2 %fusion.5 = f32[3,16,128,256]{3,2,1,0:T(8,128)} fusion(bf16[3,16,128,256]{3,1,2,0:T(8,128)(2,1)} %convolution_convert_fusion.1, bf16[3,128,128]{2,0,1:T(4,128)(2,1)S(1)} %fusion.38, bf16[3,256,256]{2,0,1:T(4,128)(2,1)} %fusion.2), kind=kOutput, calls=%fused_computation.8 | convolution fusion | flops 1209532416 | bytes 9928704 | tf_op jit(solution)/shard_map/vzxl,vjl->vzxj/dot_general | solution.py:587
  141.9 6.5 %fusion = bf16[3,16,128,256]{3,2,1,0:T(8,128)(2,1)} fusion(f32[3,16,128,256]{3,2,1,0:T(8,128)} %fusion.5, bf16[3,16,128,256]{3,2,1,0:T(8,128)(2,1)S(1)} %bitcast.98), kind=kLoop, calls=%fused_computation.2 | loop fusion | flops 4718592 | bytes 12582912 | tf_op jit(solution)/shard_map/convert_element_type | solution.py:588
  148.4 5.4 %convert_bitcast_fusion.1 = bf16[3,16,128,256]{2,3,1,0:T(8,128)(2,1)} fusion(bf16[3,16,128,256]{3,2,1,0:T(8,128)(2,1)} %fusion, bf16[3,128,128]{2,0,1:T(4,128)(2,1)S(1)} %fusion.38, bf16[3,256,256]{2,0,1:T(4,128)(2,1)} %fusion.2), kind=kOutput, calls=%fused_computation.18 | convolution fusion | flops 1211105280 | bytes 6782976 | tf_op jit(solution)/shard_map/vik,vziy->vzky/dot_general | solution.py:592
  153.8 4.9 %copy.39 = bf16[3,16,128,256]{3,1,0,2:T(8,128)(2,1)} copy(bf16[3,16,128,256]{2,3,1,0:T(8,128)(2,1)} %convert_bitcast_fusion.1) | data formatting | bytes 6291456 | tf_op jit(solution)/shard_map/convert_element_type | solution.py:594
  158.8 4.6 %convolution_bitcast_fusion.1.partial = f32[128,32,256]{2,1,0:T(8,128)} fusion(bf16[3,16,128,256]{3,1,0,2:T(8,128)(2,1)} %copy.39, bf16[3,16,32]{2,0,1:T(4,128)(2,1)S(1)} %fusion.41), kind=kOutput, calls=%fused_computation.28 | convolution fusion | flops 100663296 | bytes 7343104 | tf_op jit(solution)/shard_map/vzp,vzxy->xpy/dot_general | solution.py:595
  163.4 43.5 %renew.1 = (f32[16,32,256]{2,1,0:T(8,128)S(1)}, bf16[32,128,256]{2,1,0:T(8,128)(2,1)S(1)}) custom-call(f32[128,32,256]{2,1,0:T(8,128)} %convolution_bitcast_fusion.1.partial, f32[16,32,256]{2,1,0:T(8,128)S(1)} %copy-done.2), custom_call_target="tpu_custom_call" | custom-call | tf_op jit(solution)/shard_map/renew/pallas_call | solution.py:542
  206.9 0.8 copy-done.3
  207.7 3.1 %convolution_convert_fusion = bf16[3,16,128,256]{3,1,2,0:T(8,128)(2,1)} fusion(bf16[32,128,256]{2,1,0:T(8,128)(2,1)S(1)} %get-tuple-element.19, bf16[3,16,32]{2,0,1:T(4,128)(2,1)S(1)} %fusion.41), kind=kOutput, calls=%fused_computation.25 | convolution fusion | flops 102236160 | bytes 5245952 | tf_op jit(solution)/shard_map/vzp,pxy->vzxy/dot_general | solution.py:581
  210.8 7.2 %fusion.3 = f32[3,16,128,256]{3,2,1,0:T(8,128)} fusion(bf16[3,16,128,256]{3,1,2,0:T(8,128)(2,1)} %convolution_convert_fusion, bf16[3,128,128]{2,0,1:T(4,128)(2,1)S(1)} %fusion.38, bf16[3,256,256]{2,0,1:T(4,128)(2,1)} %fusion.2), kind=kOutput, calls=%fused_computation.6 | convolution fusion | flops 1209532416 | bytes 9928704 | tf_op jit(solution)/shard_map/vzxl,vjl->vzxj/dot_general | solution.py:587
  218.0 6.5 %fusion.1 = bf16[3,16,128,256]{3,2,1,0:T(8,128)(2,1)} fusion(f32[3,16,128,256]{3,2,1,0:T(8,128)} %fusion.3, bf16[3,16,128,256]{3,2,1,0:T(8,128)(2,1)S(1)} %bitcast.99), kind=kLoop, calls=%fused_computation.3 | loop fusion | flops 4718592 | bytes 12582912 | tf_op jit(solution)/shard_map/convert_element_type | solution.py:588
  224.5 5.4 %convert_bitcast_fusion = bf16[3,16,128,256]{2,3,1,0:T(8,128)(2,1)} fusion(bf16[3,16,128,256]{3,2,1,0:T(8,128)(2,1)} %fusion.1, bf16[3,128,128]{2,0,1:T(4,128)(2,1)S(1)} %fusion.38, bf16[3,256,256]{2,0,1:T(4,128)(2,1)} %fusion.2), kind=kOutput, calls=%fused_computation.14 | convolution fusion | flops 1211105280 | bytes 6782976 | tf_op jit(solution)/shard_map/vik,vziy->vzky/dot_general | solution.py:592
  230.0 3.9 %copy.44 = bf16[3,16,128,256]{3,1,0,2:T(8,128)(2,1)S(1)} copy(bf16[3,16,128,256]{2,3,1,0:T(8,128)(2,1)} %convert_bitcast_fusion) | data formatting | bytes 6291456 | tf_op jit(solution)/shard_map/convert_element_type | solution.py:594
  233.8 2.7 convolution_bitcast_fusion.partial
  236.5 41.9 %finish.1 = f32[16,128,256]{2,1,0:T(8,128)S(1)} custom-call(f32[128,32,256]{2,1,0:T(8,128)} %convolution_bitcast_fusion.partial, f32[16,32,256]{2,1,0:T(8,128)S(1)} %copy-done.4), custom_call_target="tpu_custom_call" | custom-call | tf_op jit(solution)/shard_map/finish/pallas_call | solution.py:542
  278.4 1.3 copy.125
  (17 shorter events, 0.2 us)
Async XLA Ops:
  4.8 8.6 %copy-start = (f32[16,128,256]{2,1,0:T(8,128)S(1)}, f32[16,128,256]{2,1,0:T(8,128)}, u32[]{:S(2)}) copy-start(f32[16,128,256]{2,1,0:T(8,128)} %estimate.1) | copy-start | bytes 6291460
  4.8 8.6 %copy-start.5 = (s32[3,128]{1,0:T(4,128)S(1)}, s32[3,128]{1,0:T(4,128)}, u32[]{:S(2)}) copy-start(s32[3,128]{1,0:T(4,128)} %dest.1) | copy-start | bytes 4612
  11.7 1.7 copy-start.1
  158.8 4.6 %copy-start.2 = (f32[16,32,256]{2,1,0:T(8,128)S(1)}, f32[16,32,256]{2,1,0:T(8,128)}, u32[]{:S(2)}) copy-start(f32[16,32,256]{2,1,0:T(8,128)} %constant_dynamic-slice_fusion.held) | copy-start | bytes 1572868
  206.9 0.8 copy-start.3
  233.8 2.7 copy-start.4
